TPU v7x, 256 devices: a whole 4x4x8 slice. The times are simulated.
256 devices in a mesh: samp: 8 (over z_hi, core), grp: 32 (over z_lo, x, y).
Axes of the slice: x: 4, y: 4, z: 8 (z_hi: 4, z_lo: 2; z = z_hi * 2 + z_lo), core: 2. Of those that a mesh axis runs over, the one named last changes fastest.
Arguments:
- volumes: bfloat16 [8, 64, 128, 16, 128], P('samp', None, 'grp'), may hold values from -6 to 6
- w_first: bfloat16 [128, 1728], replicated, may hold values from -0.15625 to 0.15625
- bias_first: float32 [128], replicated, may hold values from -4 to 4
- w_second: bfloat16 [256, 27, 128], replicated, may hold values from -0.109375 to 0.109375
- cotangent: bfloat16 [8, 256, 32, 128], P('samp', 'grp'), may hold values from -6 to 6
Outputs:
- pre_grad: bfloat16 [8, 128, 64, 4, 128], P('samp', None, 'grp')
- w2_grad: float32 [256, 27, 128], P(None, None, 'grp')
All inputs are finite; a program needn't handle non-finite values.
Results may differ from a plain program's by a relative error of at most 0.0049.
Values may be sent and summed in bfloat16 or wider, within the bound.
A program may use at most 64 MiB of HBM per device.

v0:
```python
import math

import jax
import jax.numpy as jnp
from jax import lax
from jax.sharding import PartitionSpec as P

YCELLS = 32
ZCELLS = 64


OFFSETS = (-1, 0, 1)


def shifted(block, axis, distance):
    devices = range(lax.axis_size(axis))
    route = [((i - distance) % len(devices), i) for i in devices]
    return lax.ppermute(block, axis, route)


def shift_rows(field, z_quarter, step):
    return jnp.roll(field, step * z_quarter, axis=-1)


def shift_cells(field, z_quarter, step):
    position = jnp.arange(field.shape[-1], dtype=jnp.int32) % z_quarter
    if step == 1:
        return jnp.where(
            position == 0, jnp.roll(field, 1 - z_quarter, axis=-1), jnp.roll(field, 1, axis=-1)
        )
    return jnp.where(
        position == z_quarter - 1,
        jnp.roll(field, z_quarter - 1, axis=-1),
        jnp.roll(field, -1, axis=-1),
    )


def first_patches(extended, planes, z_quarter):
    channels = extended.shape[0]
    pieces = []
    for offset_x in OFFSETS:
        plane_set = extended[:, offset_x + 1 : offset_x + 1 + 2 * planes : 2]
        for offset_y in OFFSETS:
            for offset_z in OFFSETS:
                phases = []
                for half_y in (0, 1):
                    for half_z in (0, 1):
                        along_y = 2 * half_y + offset_y
                        along_z = 2 * half_z + offset_z
                        picked = plane_set[:, :, 4 * (along_y % 4) + along_z % 4]
                        if along_y < 0:
                            picked = shift_rows(picked, z_quarter, 1)
                        if along_z < 0:
                            picked = shift_cells(picked, z_quarter, 1)
                        phases.append(picked)
                pieces.append(jnp.stack(phases, axis=2).reshape(channels, -1))
    return jnp.concatenate(pieces, axis=0)


def second_patches(extended, planes, z_quarter):
    channels = extended.shape[0]
    pieces = []
    for offset_x in OFFSETS:
        plane_set = extended[:, offset_x + 1 : offset_x + 1 + 2 * planes : 2]
        for offset_y in OFFSETS:
            for offset_z in OFFSETS:
                phase_y = 0 if offset_y == 0 else 1
                phase_z = 0 if offset_z == 0 else 1
                picked = plane_set[:, :, 2 * phase_y + phase_z]
                if offset_y < 0:
                    picked = shift_rows(picked, z_quarter, 1)
                if offset_z < 0:
                    picked = shift_cells(picked, z_quarter, 1)
                pieces.append(picked.reshape(channels, -1))
    return jnp.concatenate(pieces, axis=0)


def fold_taps(stacked, axis):
    lower_tap, middle, upper_tap = (stacked[0], stacked[1], stacked[2])
    following = jnp.roll(lower_tap, -1, axis=axis)
    return jnp.stack([middle, upper_tap + following], axis=axis + 1)


def place_taps(products, channels, planes, z_quarter):
    cells = products.shape[-1]
    stacked = products.reshape(3, 3, 3, channels, cells // (z_quarter * (YCELLS // 4)), -1)
    folded = fold_taps(stacked, 3)
    folded = folded.reshape(3, 3, channels, 2 * planes, -1)
    by_rows = [folded[1], folded[2] + shift_rows(folded[0], z_quarter, -1)]
    phases = []
    for row_part in by_rows:
        phases.append(row_part[1])
        phases.append(row_part[2] + shift_cells(row_part[0], z_quarter, -1))
    return jnp.stack(phases, axis=2)


def slope_of(pre_act):
    sigmoid_pre = jax.nn.sigmoid(pre_act)
    return sigmoid_pre * (1.0 + pre_act * (1.0 - sigmoid_pre))


def on_device(volumes, w_first, bias_first, w_second, cotangent):
    z_quarter = ZCELLS // 4
    volume_block = volumes[0]
    in_planes = volume_block.shape[1]
    rim_plane = shifted(volume_block[:, -1:], "grp", 1)
    patches_first = first_patches(
        jnp.concatenate([rim_plane, volume_block], axis=1), in_planes // 2, z_quarter
    )
    pre_act = (
        jnp.dot(w_first, patches_first, preferred_element_type=jnp.float32) + bias_first[:, None]
    )
    hidden = jax.nn.silu(pre_act).astype(jnp.bfloat16)
    out_channels = hidden.shape[0]
    mid_planes = in_planes // 2
    groups = lax.axis_size("grp")
    filters = w_second.shape[0]
    channel_share = out_channels // groups
    start_channel = lax.axis_index("grp") * channel_share
    quarter_cells = YCELLS // 4 * z_quarter
    contract_rows = (((1,), (1,)), ((), ()))
    contract_first = (((0,), (0,)), ((), ()))
    columns = lax.all_to_all(
        hidden.reshape(out_channels, mid_planes, -1), "grp", split_axis=0, concat_axis=1, tiled=True
    )
    whole_planes = columns.shape[1]
    column_volume = columns.reshape(channel_share, whole_planes, 4, quarter_cells)
    patches_second = second_patches(
        jnp.concatenate([column_volume[:, -1:], column_volume], axis=1),
        whole_planes // 2,
        z_quarter,
    )
    every_filter = lax.all_gather(cotangent[0], "grp", axis=0, tiled=True).reshape(filters, -1)
    w_share = lax.dynamic_slice_in_dim(w_second, start_channel, channel_share, 2).reshape(
        filters, -1
    )
    partial_grad = lax.dot_general(
        every_filter, patches_second, contract_rows, preferred_element_type=jnp.float32
    )
    partial_grad = partial_grad.reshape(filters, 27, channel_share)
    products = lax.dot_general(
        w_share, every_filter, contract_first, preferred_element_type=jnp.float32
    )
    column_grad = place_taps(products, channel_share, whole_planes // 2, z_quarter).astype(
        jnp.bfloat16
    )
    hidden_grad = lax.all_to_all(
        column_grad.reshape(channel_share, whole_planes, -1),
        "grp",
        split_axis=1,
        concat_axis=0,
        tiled=True,
    )
    hidden_grad = hidden_grad.reshape(out_channels, -1)
    pre_grad = (hidden_grad.astype(jnp.float32) * slope_of(pre_act)).astype(jnp.bfloat16)
    total_cells = (
        lax.axis_size("samp") * volumes.shape[0] * groups * (in_planes // 4) * quarter_cells
    )
    w2_grad = lax.psum(partial_grad, "samp") * (1.0 / math.sqrt(total_cells))
    return (pre_grad.reshape(1, out_channels, mid_planes, 4, quarter_cells), w2_grad)


def solution(mesh):
    placed = (P("samp", None, "grp", None, None), P(), P(), P(), P("samp", "grp", None, None))
    return jax.shard_map(
        on_device,
        mesh=mesh,
        in_specs=placed,
        out_specs=(P("samp", None, "grp", None, None), P(None, None, "grp")),
        check_vma=False,
    )
```

profile of v0, /device:TPU:1, one launch (start us, length us, event | category | flops | bytes accessed | tf_op | source)
XLA Modules:
  0.0 311.2 jit_solution(1999037663801578122)
XLA Ops:
  7.2 2.0 copy.344
  10.0 2.1 collective-permute-start
  41.3 1.8 constant_dynamic-slice_fusion
  43.4 1.6 maximum_select_fusion.15
  45.1 1.7 pad_maximum_fusion.18
  49.2 1.6 reshape.1191
  56.1 2.1 copy.175
  66.4 1.7 maximum_select_fusion.14
  70.0 1.6 reshape.1190
  71.6 1.7 pad_maximum_fusion.9
  74.1 1.6 reshape.1184
  78.2 1.6 reshape.1181
  81.7 1.6 reshape.1182
  84.1 1.6 reshape.1183
  95.0 1.7 reshape.1201
  96.7 1.7 pad_maximum_fusion.27
  99.2 1.7 copy.225
  101.9 1.6 constant_dynamic-update-slice_fusion.26
  108.2 1.6 constant_dynamic-update-slice_fusion.22
  111.3 1.6 constant_dynamic-update-slice_fusion.20
  112.9 1.6 constant_dynamic-update-slice_fusion.19
  125.5 24.8 %all-gather.3.cloned.1.call-done = bf16[1,256,32,128]{3,2,0,1:T(8,128)(2,1)} async-done(((bf16[1,8,32,128]{3,2,0,1:T(8,128)(2,1)}), bf16[1,256,32,128]{3,2,0,1:T(8,128)(2,1)}) %all-gather.3.cloned.1.call-update) | async-done | bytes 2097168 | tf_op jit(solution)/shard_map/all_gather | solution.py:133
  150.4 2.4 fusion.2
  156.8 6.7 %all-to-all-start = ((bf16[4,64,512]{2,0,1:T(4,128)(2,1)}), bf16[4,64,512]{2,0,1:T(4,128)(2,1)S(1)}, u32[]{:S(2)}, u32[]{:S(2)}) async-start(bf16[4,64,512]{2,0,1:T(4,128)(2,1)} %reshape.1222), calls=%async_computation | async-start | bytes 524288 | tf_op jit(solution)/shard_map/all_to_all | solution.py:147
  167.4 3.9 %all-to-all-done = bf16[4,64,512]{2,0,1:T(4,128)(2,1)S(1)} async-done(((bf16[4,64,512]{2,0,1:T(4,128)(2,1)}), bf16[4,64,512]{2,0,1:T(4,128)(2,1)S(1)}, u32[]{:S(2)}, u32[]{:S(2)}) %all-to-all-start) | async-done | bytes 262176 | tf_op jit(solution)/shard_map/all_to_all | solution.py:147
  172.0 3.3 %multiply_convert_fusion = (bf16[128,1024]{0,1:T(8,128)(2,1)S(1)}, bf16[128,1024]{0,1:T(8,128)(2,1)S(1)}) fusion(f32[128,1024]{0,1:T(8,128)S(1)} %copy.231, f32[128]{0:T(128)S(1)} %copy-done.42, bf16[1728,1024]{1,0:T(8,128)(2,1)} %constant_dynamic-update-slice_fusion, bf16[128,1728]{0,1:T(8,128)(2,1)} %param.6), kind=kOutput, calls=%fused_computation.22 | convolution fusion | flops 454557696 | bytes 5030400 | tf_op jit(solution)/shard_map/dot_general | solution.py:111
  176.1 3.9 %all-to-all-start.1 = ((bf16[128,2,512]{2,1,0:T(2,128)(2,1)}), bf16[128,2,512]{2,1,0:T(2,128)(2,1)S(1)}, u32[]{:S(2)}, u32[]{:S(2)}) async-start(bf16[128,2,512]{2,1,0:T(2,128)(2,1)} %copy.232), calls=%async_computation.1 | async-start | bytes 524288 | tf_op jit(solution)/shard_map/all_to_all | solution.py:123
  180.1 7.9 %all-to-all-done.1 = bf16[128,2,512]{2,1,0:T(2,128)(2,1)S(1)} async-done(((bf16[128,2,512]{2,1,0:T(2,128)(2,1)}), bf16[128,2,512]{2,1,0:T(2,128)(2,1)S(1)}, u32[]{:S(2)}, u32[]{:S(2)}) %all-to-all-start.1) | async-done | bytes 262176 | tf_op jit(solution)/shard_map/all_to_all | solution.py:123
  201.9 6.0 %concatenate.837 = bf16[108,4096]{1,0:T(8,128)(2,1)S(1)} concatenate(bf16[4,4096]{1,0:T(4,128)(2,1)S(1)} %get-tuple-element.169, bf16[4,4096]{1,0:T(4,128)(2,1)S(1)} %bitcast.581, bf16[4,4096]{1,0:T(4,128)(2,1)S(1)} %bitcast.580, bf16[4,4096]{1,0:T(4,128)(2,1)S(1)} %get-tuple-element.162, bf16[4,4096]{1,0:T(4,128)(2,1)} %bitcast.585, bf16[4,4096]{1,0:T(4,128)(2,1)S(1)} %bitcast.584, ...), dimensions={0} | concatenate | bytes 1769472 | tf_op jit(solution)/shard_map/concatenate | solution.py:75
  207.9 2.5 fusion.7
  211.9 90.8 %all-reduce.2.cloned.1.call-done = f32[256,27,4]{0,2,1:T(4,128)} async-done(((f32[256,27,4]{0,2,1:T(4,128)}), f32[256,27,4]{0,2,1:T(4,128)}) %all-reduce.2.cloned.1.call-update) | async-done | bytes 110608 | tf_op jit(solution)/shard_map/psum | solution.py:159
  302.8 1.6 broadcast_multiply_fusion
  (376 shorter events, 106.2 us)
Async XLA Ops:
  7.2 34.0 %copy-start = (bf16[256,27,128]{2,0,1:T(8,128)(2,1)S(1)}, bf16[256,27,128]{2,0,1:T(8,128)(2,1)}, u32[]{:S(2)}) copy-start(bf16[256,27,128]{2,0,1:T(8,128)(2,1)} %param.8) | copy-start | bytes 5308420
  7.2 143.2 %all-gather.3.cloned.1.call-start = ((), (), s32[]{:S(2)}) async-start(), calls=%async_computation.3 | async-start | bytes 2162688 | tf_op jit(solution)/shard_map/all_gather | solution.py:133
  10.0 49.1 %collective-permute-start = (bf16[64,1,16,128]{3,0,1,2:T(8,128)(2,1)}, bf16[64,1,16,128]{3,0,1,2:T(8,128)(2,1)}, u32[]{:S(2)}, u32[]{:S(2)}) collective-permute-start(bf16[64,1,16,128]{3,0,1,2:T(8,128)(2,1)} %slice.1082), channel_id=1, source_target_pairs={{31,0},{0,1},{1,2},{2,3},{3,4},{4,5},{5,6},{6,7},{7,8},{8,9},{9,10... | collective-permute-start | bytes 786440 | tf_op jit(solution)/shard_map/ppermute | solution.py:18
  58.2 5.6 %copy-start.19 = (bf16[64,2,1,127]{3,0,1,2:T(8,128)(2,1)S(1)}, bf16[64,2,1,127]{3,0,1,2:T(8,128)(2,1)}, u32[]{:S(2)}) copy-start(bf16[64,2,1,127]{3,0,1,2:T(8,128)(2,1)} %get-tuple-element.201) | copy-start | bytes 97540
  58.9 5.6 %copy-start.24 = (bf16[64,2,1,127]{3,0,1,2:T(8,128)(2,1)S(1)}, bf16[64,2,1,127]{3,0,1,2:T(8,128)(2,1)}, u32[]{:S(2)}) copy-start(bf16[64,2,1,127]{3,0,1,2:T(8,128)(2,1)} %slice_bitcast_fusion.11) | copy-start | bytes 97540
  58.9 5.6 %copy-start.25 = (bf16[64,2,1,113]{3,0,1,2:T(8,128)(2,1)S(1)}, bf16[64,2,1,113]{3,0,1,2:T(8,128)(2,1)}, u32[]{:S(2)}) copy-start(bf16[64,2,1,113]{3,0,1,2:T(8,128)(2,1)} %slice_bitcast_fusion.14) | copy-start | bytes 86788
  58.9 5.6 %copy-start.38 = (bf16[64,2,1,1]{3,0,1,2:T(8,128)(2,1)S(1)}, bf16[64,2,1,1]{3,0,1,2:T(8,128)(2,1)}, u32[]{:S(2)}) copy-start(bf16[64,2,1,1]{3,0,1,2:T(8,128)(2,1)} %get-tuple-element.149) | copy-start | bytes 772
  59.0 6.3 %copy-start.15 = (bf16[64,2,1,128]{3,0,1,2:T(8,128)(2,1)S(1)}, bf16[64,2,1,128]{3,0,1,2:T(8,128)(2,1)}, u32[]{:S(2)}) copy-start(bf16[64,2,1,128]{3,0,1,2:T(8,128)(2,1)} %get-tuple-element.33) | copy-start | bytes 98308
  59.0 6.3 %copy-start.16 = (bf16[64,2,1,128]{3,0,1,2:T(8,128)(2,1)S(1)}, bf16[64,2,1,128]{3,0,1,2:T(8,128)(2,1)}, u32[]{:S(2)}) copy-start(bf16[64,2,1,128]{3,0,1,2:T(8,128)(2,1)} %get-tuple-element.53) | copy-start | bytes 98308
  59.0 6.3 %copy-start.17 = (bf16[64,2,1,128]{3,0,1,2:T(8,128)(2,1)S(1)}, bf16[64,2,1,128]{3,0,1,2:T(8,128)(2,1)}, u32[]{:S(2)}) copy-start(bf16[64,2,1,128]{3,0,1,2:T(8,128)(2,1)} %get-tuple-element.54) | copy-start | bytes 98308
  59.0 6.3 %copy-start.18 = (bf16[64,2,1,128]{3,0,1,2:T(8,128)(2,1)S(1)}, bf16[64,2,1,128]{3,0,1,2:T(8,128)(2,1)}, u32[]{:S(2)}) copy-start(bf16[64,2,1,128]{3,0,1,2:T(8,128)(2,1)} %get-tuple-element.55) | copy-start | bytes 98308
  59.0 6.3 %copy-start.40 = (bf16[64,2,1,128]{3,0,1,2:T(8,128)(2,1)S(1)}, bf16[64,2,1,128]{3,0,1,2:T(8,128)(2,1)}, u32[]{:S(2)}) copy-start(bf16[64,2,1,128]{3,0,1,2:T(8,128)(2,1)} %get-tuple-element.214) | copy-start | bytes 98308
  59.1 6.3 %copy-start.41 = (bf16[64,2,1,128]{3,0,1,2:T(8,128)(2,1)S(1)}, bf16[64,2,1,128]{3,0,1,2:T(8,128)(2,1)}, u32[]{:S(2)}) copy-start(bf16[64,2,1,128]{3,0,1,2:T(8,128)(2,1)} %get-tuple-element.215) | copy-start | bytes 98308
  60.2 6.2 %copy-start.23 = (bf16[64,2,1,127]{3,0,1,2:T(8,128)(2,1)S(1)}, bf16[64,2,1,127]{3,0,1,2:T(8,128)(2,1)}, u32[]{:S(2)}) copy-start(bf16[64,2,1,127]{3,0,1,2:T(8,128)(2,1)} %maximum_bitcast_fusion.2) | copy-start | bytes 97540
  77.4 19.3 %copy-start.14 = (bf16[64,2,1,128]{3,0,1,2:T(8,128)(2,1)S(1)}, bf16[64,2,1,128]{3,0,1,2:T(8,128)(2,1)}, u32[]{:S(2)}) copy-start(bf16[64,2,1,128]{3,0,1,2:T(8,128)(2,1)} %get-tuple-element.41) | copy-start | bytes 98308
  90.1 25.9 %copy-start.7 = (bf16[64,1024]{1,0:T(8,128)(2,1)S(1)}, bf16[64,1024]{1,0:T(8,128)(2,1)}, u32[]{:S(2)}) copy-start(bf16[64,1024]{1,0:T(8,128)(2,1)} %reshape.1190) | copy-start | bytes 393220
  90.9 25.8 %copy-start.5 = (bf16[64,1024]{1,0:T(8,128)(2,1)S(1)}, bf16[64,1024]{1,0:T(8,128)(2,1)}, u32[]{:S(2)}) copy-start(bf16[64,1024]{1,0:T(8,128)(2,1)} %reshape.1191) | copy-start | bytes 393220
  91.8 27.8 %copy-start.2 = (bf16[64,1024]{1,0:T(8,128)(2,1)S(1)}, bf16[64,1024]{1,0:T(8,128)(2,1)}, u32[]{:S(2)}) copy-start(bf16[64,1024]{1,0:T(8,128)(2,1)} %reshape.1194) | copy-start | bytes 393220
  92.6 27.7 %copy-start.4 = (bf16[64,1024]{1,0:T(8,128)(2,1)S(1)}, bf16[64,1024]{1,0:T(8,128)(2,1)}, u32[]{:S(2)}) copy-start(bf16[64,1024]{1,0:T(8,128)(2,1)} %reshape.1195) | copy-start | bytes 393220
  93.4 28.2 %copy-start.3 = (bf16[64,1024]{1,0:T(8,128)(2,1)S(1)}, bf16[64,1024]{1,0:T(8,128)(2,1)}, u32[]{:S(2)}) copy-start(bf16[64,1024]{1,0:T(8,128)(2,1)} %reshape.1197) | copy-start | bytes 393220
  94.3 28.6 %copy-start.6 = (bf16[64,1024]{1,0:T(8,128)(2,1)S(1)}, bf16[64,1024]{1,0:T(8,128)(2,1)}, u32[]{:S(2)}) copy-start(bf16[64,1024]{1,0:T(8,128)(2,1)} %reshape.1199) | copy-start | bytes 393220
  95.0 28.5 %copy-start.1 = (bf16[64,1024]{1,0:T(8,128)(2,1)S(1)}, bf16[64,1024]{1,0:T(8,128)(2,1)}, u32[]{:S(2)}) copy-start(bf16[64,1024]{1,0:T(8,128)(2,1)} %reshape.1200) | copy-start | bytes 393220
  98.4 52.0 %copy-start.13 = (bf16[256,108]{0,1:T(8,128)(2,1)S(1)}, bf16[256,108]{0,1:T(8,128)(2,1)}, u32[]{:S(2)}) copy-start(bf16[256,108]{0,1:T(8,128)(2,1)} %reshape.1179) | copy-start | bytes 165892
  101.8 19.1 %copy-start.10 = (bf16[64,1024]{1,0:T(8,128)(2,1)S(1)}, bf16[64,1024]{1,0:T(8,128)(2,1)}, u32[]{:S(2)}) copy-start(bf16[64,1024]{1,0:T(8,128)(2,1)} %reshape.1196) | copy-start | bytes 393220
  101.9 20.4 %copy-start.9 = (bf16[64,1024]{1,0:T(8,128)(2,1)S(1)}, bf16[64,1024]{1,0:T(8,128)(2,1)}, u32[]{:S(2)}) copy-start(bf16[64,1024]{1,0:T(8,128)(2,1)} %reshape.1198) | copy-start | bytes 393220
  101.9 22.4 %copy-start.8 = (bf16[64,1024]{1,0:T(8,128)(2,1)S(1)}, bf16[64,1024]{1,0:T(8,128)(2,1)}, u32[]{:S(2)}) copy-start(bf16[64,1024]{1,0:T(8,128)(2,1)} %reshape.1201) | copy-start | bytes 393220
  101.9 23.0 %copy-start.11 = (bf16[64,1024]{1,0:T(8,128)(2,1)S(1)}, bf16[64,1024]{1,0:T(8,128)(2,1)}, u32[]{:S(2)}) copy-start(bf16[64,1024]{1,0:T(8,128)(2,1)} %reshape.1202) | copy-start | bytes 393220
  155.1 9.1 %copy-start.12 = (bf16[64,2,4,128]{3,0,1,2:T(8,128)(2,1)S(1)}, bf16[64,2,4,128]{3,0,1,2:T(8,128)(2,1)}, u32[]{:S(2)}) copy-start(bf16[64,2,4,128]{3,0,1,2:T(8,128)(2,1)} %get-tuple-element.119) | copy-start | bytes 393220
  156.8 14.5 %all-to-all-start = ((bf16[4,64,512]{2,0,1:T(4,128)(2,1)}), bf16[4,64,512]{2,0,1:T(4,128)(2,1)S(1)}, u32[]{:S(2)}, u32[]{:S(2)}) async-start(bf16[4,64,512]{2,0,1:T(4,128)(2,1)} %reshape.1222), calls=%async_computation | async-start | bytes 524288 | tf_op jit(solution)/shard_map/all_to_all | solution.py:147
  163.5 8.4 %copy-start.42 = (f32[128]{0:T(128)S(1)}, f32[128]{0:T(128)}, u32[]{:S(2)}) copy-start(f32[128]{0:T(128)} %param.7) | copy-start | bytes 1540
  176.1 11.9 %all-to-all-start.1 = ((bf16[128,2,512]{2,1,0:T(2,128)(2,1)}), bf16[128,2,512]{2,1,0:T(2,128)(2,1)S(1)}, u32[]{:S(2)}, u32[]{:S(2)}) async-start(bf16[128,2,512]{2,1,0:T(2,128)(2,1)} %copy.232), calls=%async_computation.1 | async-start | bytes 524288 | tf_op jit(solution)/shard_map/all_to_all | solution.py:123
  180.0 122.8 %all-reduce.2.cloned.1.call-start = ((), (), s32[]{:S(2)}) async-start(), calls=%async_computation.2 | async-start | bytes 221184 | tf_op jit(solution)/shard_map/psum | solution.py:159
  (16 other events, 53.1 us)
Sparse Core Ops, SparseCore 0:
  12.2 138.0 all-gather.2
  211.2 91.5 all-reduce.1
where the time goes:
time: 313 us; the launch traced here: 311 us
  waiting for transfers between devices  128 us (41%)
  local copies, waits for them, and re-layouts  122 us (39%)
  other arithmetic  25.7 us (8%)
  between operations  15.4 us (5%)
  starting transfers between devices  12.8 us (4%)
  matrix products  8.2 us (3%)
    psum x1, waiting for transfers between devices, on_device(): w2_grad = lax.psum(partial_grad, 'samp') * (1.0 / math.sqrt(total_cells))  90.8 us
    unnamed x148, local copies, waits for them, and re-layouts  35.8 us
    all_gather x1, waiting for transfers between devices, on_device(): lax.all_gather(cotangent[0], 'grp', axis=0, tiled=True).reshape(filters, -1)  24.8 us
    reshape x27, local copies, waits for them, and re-layouts, first_patches(): pieces.append(jnp.stack(phases, axis=2).reshape(channels, -1))  23.9 us
    another operation x27, local copies, waits for them, and re-layouts, first_patches(): pieces.append(jnp.stack(phases, axis=2).reshape(channels, -1))  13.2 us
    concatenate x23, local copies, waits for them, and re-layouts, shift_cells(): jnp.roll(field, 1, axis=-1)  11.4 us
    another operation x15, other arithmetic, first_patches(): pieces.append(jnp.stack(phases, axis=2).reshape(channels, -1))  11.4 us
    concatenate x23, local copies, waits for them, and re-layouts, shift_cells(): jnp.roll(field, 1 - z_quarter, axis=-1)  10.2 us
  transfers between devices with their start and end apart: 5, of which 4 were waited for; matrix products, arithmetic and copies ran while one was open for 38% of the time, Pallas kernels for 0%

commit v1 on v0

v1 whole, which is shorter than its diff:
```python
import functools
import math

import jax
import jax.numpy as jnp
from jax import lax
from jax.experimental import pallas as pl
from jax.experimental.pallas import tpu as pltpu
from jax.sharding import PartitionSpec as P

MESH = pl.DeviceIdType.MESH
F32 = jnp.float32
BF16 = jnp.bfloat16

CIN = 64
CH = 128
FILT = 256
HALF = 128
LANES = 128
ZQ = 16
GRP = 32
SAMP = 8
TAPS = 27
COMBOS = [(b, e) for b in (-1, 0, 1) for e in (-1, 0, 1)]
PHASES = [(0, 0), (0, 1), (1, 0), (1, 1)]
TAP_ORDER = [t for n in range(9) for t in (18 + n, n)] + [9 + n for n in range(9)]
SLOTS = 28
ROWS_A = 64
ROWS_B = 48
ROWS = ROWS_A + ROWS_B


def lane_index(shape):
    return lax.broadcasted_iota(jnp.int32, shape, len(shape) - 1)


def y_before(x):
    return pltpu.roll(x, ZQ, 1)


def z_before(x):
    first = lane_index(x.shape) % ZQ == 0
    return jnp.where(first, pltpu.roll(x, LANES + 1 - ZQ, 1), pltpu.roll(x, 1, 1))


def row_y_after(x):
    return jnp.concatenate([x[ZQ:], x[:ZQ]], axis=0)


def row_z_after(x):
    rows = x.shape[0]
    last = lax.broadcasted_iota(jnp.int32, x.shape, 0) % ZQ == ZQ - 1
    return jnp.where(last, pltpu.roll(x, ZQ - 1, 0), pltpu.roll(x, rows - 1, 0))


def kernel(
    vol, w1t, bias, w2, cot,
    pre_out, w2_out,
    vbuf, w1tv, w1s, biasv, w2v, cotv, cstg, cstage, crecv, cotf, cpart,
    perm, tn, ty, tz, tyz, pre_s, act_own, act_part, carry, send_buf, recv_buf,
    acc_s, zrecv, fin, cvar, pgf,
    lsem, vsem, halo_sem, cot_sem, cx_sem, act_sem, rs_sem, z_sem, ag_sem,
):
    me = lax.axis_index("grp")
    samp = lax.axis_index("samp")
    core = lax.rem(samp, 2)
    zhi = lax.div(samp, 2)
    other = samp + 1 - 2 * core

    ld_cot = pltpu.make_async_copy(cot, cotv, lsem.at[0])
    ld_w1 = pltpu.make_async_copy(w1t, w1tv, lsem.at[1])
    ld_bias = pltpu.make_async_copy(bias, biasv, lsem.at[2])
    ld_w2 = pltpu.make_async_copy(w2, w2v, lsem.at[3])
    ld_vol = [pltpu.make_async_copy(vol.at[:, x], vbuf.at[x + 1], vsem.at[x]) for x in range(4)]
    ld_cot.start()
    ld_w1.start()
    ld_bias.start()
    for x in (1, 2, 3, 0):
        ld_vol[x].start()
    ld_w2.start()

    barrier = pltpu.get_barrier_semaphore()

    def greet_grp(k, _):
        pl.semaphore_signal(
            barrier, inc=1, device_id={"grp": lax.rem(me + k, GRP)}, device_id_type=MESH
        )
        return 0

    def greet_samp(k, _):
        pl.semaphore_signal(
            barrier, inc=1, device_id={"samp": lax.rem(samp + k, SAMP)}, device_id_type=MESH
        )
        return 0

    lax.fori_loop(1, GRP, greet_grp, 0)
    lax.fori_loop(1, SAMP, greet_samp, 0)

    ld_cot.wait()
    for f in range(8):
        x = cotv[f].astype(F32)
        cstg[pl.ds(f, GRP, stride=16), :] = x
        cstg[pl.ds(8 + f, GRP, stride=16), :] = jnp.concatenate([x[1:], x[:1]], axis=0)
    cstage[...] = cstg[...].reshape(GRP, 16, LANES).astype(BF16)

    pl.semaphore_wait(barrier, GRP - 1 + SAMP - 1)

    halo = pltpu.make_async_remote_copy(
        src_ref=vol.at[:, 3], dst_ref=vbuf.at[0],
        send_sem=halo_sem.at[0], recv_sem=halo_sem.at[1],
        device_id={"grp": lax.rem(me + 1, GRP)}, device_id_type=MESH,
    )

    def send_cot(k, _):
        dest = lax.rem(me + k, GRP)
        pltpu.make_async_remote_copy(
            src_ref=cstage.at[dest], dst_ref=crecv.at[me],
            send_sem=cot_sem.at[0], recv_sem=cot_sem.at[1],
            device_id={"grp": dest}, device_id_type=MESH,
        ).start()
        return 0

    lax.fori_loop(1, GRP, send_cot, 0)
    halo.start()
    crecv[me] = cstage[me]

    ld_w1.wait()
    ld_bias.wait()
    w1s[...] = jnp.transpose(w1tv[...])
    bias_rows = jnp.transpose(jnp.broadcast_to(biasv[...], (CH, CH)))
    row = lax.broadcasted_iota(jnp.int32, (256, 256), 0)
    col = lax.broadcasted_iota(jnp.int32, (256, 256), 1)
    perm[...] = jnp.where(col == (row % 16) * 16 + row // 16, 1.0, 0.0).astype(BF16)

    def by_phase(x):
        for blk in range(4):
            rows = vbuf[x, 16 * blk : 16 * blk + 16].reshape(256, LANES)
            moved = jnp.dot(perm[...], rows, preferred_element_type=F32)
            here = slice(16 * blk, 16 * blk + 16)
            tn[x, :, here, :] = moved.reshape(16, 16, LANES).astype(BF16)
            ty[x, :, here, :] = y_before(moved[192:256]).reshape(4, 16, LANES).astype(BF16)
            ends = jnp.concatenate([moved[64 * r + 48 : 64 * r + 64] for r in range(4)], axis=0)
            ends = z_before(ends)
            tz[x, :, here, :] = ends.reshape(4, 16, LANES).astype(BF16)
            tyz[x, here, :] = y_before(ends[48:64]).astype(BF16)

    def patch(x, qy, qz, b, e):
        along_y, along_z = 2 * qy + b, 2 * qz + e
        ry, rz = along_y % 4, along_z % 4
        if along_y < 0 and along_z < 0:
            return tyz[x]
        if along_y < 0:
            return ty[x, rz]
        if along_z < 0:
            return tz[x, ry]
        return tn[x, 4 * ry + rz]

    def first_layer(i):
        for pair in (0, 1):
            columns = []
            for q in (2 * pair, 2 * pair + 1):
                qy, qz = PHASES[q]
                columns.append(
                    jnp.concatenate(
                        [patch(2 * i + a, qy, qz, b, e) for a in range(3) for b, e in COMBOS], axis=0
                    )
                )
            patches = jnp.concatenate(columns, axis=1)
            pre = jnp.dot(w1s[...], patches, preferred_element_type=F32)
            for h in (0, 1):
                part = pre[:, LANES * h : LANES * (h + 1)] + bias_rows
                pre_s[i, 2 * pair + h] = part
                act_own[i, 2 * pair + h] = (part / (1.0 + jnp.exp(-part))).astype(BF16)

    def exchange_act(i):
        return pltpu.make_async_remote_copy(
            src_ref=act_own.at[i], dst_ref=act_part.at[i],
            send_sem=act_sem.at[0, i], recv_sem=act_sem.at[1, i],
            device_id={"samp": other}, device_id_type=MESH,
        )

    for x in (1, 2, 3):
        ld_vol[x].wait()
        by_phase(x + 1)
    first_layer(1)
    act_copy = [exchange_act(0), exchange_act(1)]
    act_copy[1].start()

    pltpu.make_async_copy(
        crecv.at[pl.ds(0, GRP - 1)], crecv.at[pl.ds(0, GRP - 1)], cot_sem.at[1]
    ).wait()
    got = crecv[...].astype(F32)
    for p in (0, 1):
        cotf[p] = got[:, 8 * p : 8 * p + 8].reshape(FILT, LANES).astype(BF16)
    cx = pltpu.make_async_remote_copy(
        src_ref=cotf.at[:, pl.ds(pl.multiple_of(HALF * (1 - core), HALF), HALF), :], dst_ref=cpart,
        send_sem=cx_sem.at[0], recv_sem=cx_sem.at[1],
        device_id={"samp": other}, device_id_type=MESH,
    )
    cx.start()

    ld_vol[0].wait()
    by_phase(1)

    my_half = pl.ds(pl.multiple_of(HALF * core, HALF), HALF)

    def second_patch(i, n):
        b, e = COMBOS[n]
        phase = 2 * (b != 0) + (e != 0)
        parts = []
        for ref in (act_own, act_part):
            x = ref[i, phase]
            if b < 0 or e < 0:
                x = x.astype(F32)
                if e < 0:
                    x = z_before(x)
                if b < 0:
                    x = y_before(x)
                x = x.astype(BF16)
            parts.append(x)
        return jnp.concatenate(parts, axis=1)

    contract = (((1,), (1,)), ((), ()))

    def pack(group, taps):
        low = lax.broadcasted_iota(jnp.int32, (16, 8, LANES), 1) < 4
        t = [x.reshape(16, 8, LANES) for x in taps]
        turned = [pltpu.roll(x, 4, 1) for x in t]
        even = [jnp.where(low, t[j], turned[j + 1]) for j in (0, 2)]
        odd = [jnp.where(low, turned[j], t[j + 1]) for j in (0, 2)]
        rows = slice(16 * group, 16 * group + 16)
        send_buf[:, 0, rows, :] = jnp.concatenate(even, axis=1).astype(BF16)
        send_buf[:, 1, rows, :] = jnp.concatenate(odd, axis=1).astype(BF16)

    def send_chunk(which):
        rows = pl.ds(0, ROWS_A) if which == 0 else pl.ds(ROWS_A, ROWS_B)

        def body(k, _):
            dest = lax.rem(me + k, GRP)
            pltpu.make_async_remote_copy(
                src_ref=send_buf.at[lax.div(dest, 2), lax.rem(dest, 2), rows],
                dst_ref=recv_buf[which].at[k - 1],
                send_sem=rs_sem.at[0, which], recv_sem=rs_sem.at[1, which],
                device_id={"grp": dest}, device_id_type=MESH,
            ).start()
            return 0

        lax.fori_loop(1, GRP, body, 0)

    def cot_rhs(p):
        return jnp.concatenate([cotf[p, my_half, :], cpart[p]], axis=1)

    act_copy[1].wait_recv()
    cx.wait_recv()
    rhs_both = jnp.concatenate([cot_rhs(0), cot_rhs(1)], axis=0)
    held = []
    for n in range(9):
        d = lax.dot_general(second_patch(1, n), rhs_both, contract, preferred_element_type=F32)
        held += [d[:, :LANES], d[:, LANES:]]
        if len(held) == 4:
            pack(n // 2, held)
            held = []
    carry[0] = held[0]
    carry[1] = held[1]
    send_chunk(0)

    halo.wait_recv()
    by_phase(0)
    first_layer(0)
    act_copy[0].start()

    for p in (0, 1):
        turned = jnp.transpose(cotf[p].astype(F32))
        cvar[p, 0] = turned.astype(BF16)
        cvar[p, 2] = row_y_after(turned).astype(BF16)
        after = row_z_after(turned)
        cvar[p, 1] = after.astype(BF16)
        cvar[p, 3] = row_y_after(after).astype(BF16)

    act_copy[0].wait_recv()
    rhs_one = cot_rhs(0)
    held = [carry[0], carry[1]]
    group = 4
    for n in range(9):
        held.append(
            lax.dot_general(second_patch(0, n), rhs_one, contract, preferred_element_type=F32)
        )
        if len(held) == 4:
            pack(group, held)
            group += 1
            held = []
    pack(group, held + [jnp.zeros((CH, LANES), F32)] * (4 - len(held)))
    send_chunk(1)

    ld_w2.wait()
    for i in (0, 1):
        for q, (qy, qz) in enumerate(PHASES):
            left, right = [], []
            for a, p in ((0, 0),) if i == 0 else ((1, 0), (-1, 1)):
                for b, sy in ((0, 0),) if qy == 0 else ((1, 0), (-1, 1)):
                    for e, sz in ((0, 0),) if qz == 0 else ((1, 0), (-1, 1)):
                        left.append(cvar[p, 2 * sy + sz])
                        right.append(w2v[9 * (a + 1) + 3 * (b + 1) + e + 1])
            grad = jnp.dot(
                jnp.concatenate(left, axis=1),
                jnp.concatenate(right, axis=0),
                preferred_element_type=F32,
            )
            grad = jnp.transpose(grad.astype(BF16).astype(F32))
            z = pre_s[i, q]
            g = 1.0 / (1.0 + jnp.exp(-z))
            pgf[pl.ds(4 * i + q, CH, stride=8), :] = grad * (g * (1.0 + z * (1.0 - g)))
    pre_out[...] = pgf[...].reshape(CH, 8, LANES).astype(BF16)

    mine = send_buf.at[lax.div(me, 2), lax.rem(me, 2)]
    for which, rows in ((0, pl.ds(0, ROWS_A)), (1, pl.ds(ROWS_A, ROWS_B))):
        pltpu.make_async_copy(recv_buf[which], recv_buf[which], rs_sem.at[1, which]).wait()
        acc_s[rows, :] = lax.fori_loop(
            0,
            GRP - 1,
            lambda j, acc: acc + recv_buf[which][j].astype(F32),
            mine[rows, :].astype(F32),
        )
    acc_s[pl.ds(ROWS, 128 - ROWS), :] = jnp.zeros((128 - ROWS, LANES), F32)

    def z_peer(k):
        return lax.rem(zhi + k, 4)

    z_copies = []
    for k in (1, 2, 3):
        peer = z_peer(k)
        z_copies.append(
            pltpu.make_async_remote_copy(
                src_ref=acc_s.at[pl.ds(pl.multiple_of(32 * peer, 32), 32)], dst_ref=zrecv.at[k - 1],
                send_sem=z_sem.at[0, k - 1], recv_sem=z_sem.at[1, k - 1],
                device_id={"samp": 2 * peer + core}, device_id_type=MESH,
            )
        )
        z_copies[-1].start()
    for c in z_copies:
        c.wait_recv()
    scale = 1.0 / math.sqrt(32768)
    my_rows = pl.ds(pl.multiple_of(32 * zhi, 32), 32)
    fin_rows = pl.ds(pl.multiple_of(128 * core + 32 * zhi, 32), 32)
    fin[fin_rows, :] = (acc_s[my_rows, :] + zrecv[0] + zrecv[1] + zrecv[2]) * scale

    def send_fin(k, _):
        pltpu.make_async_remote_copy(
            src_ref=fin.at[fin_rows], dst_ref=fin.at[fin_rows],
            send_sem=ag_sem.at[0], recv_sem=ag_sem.at[1],
            device_id={"samp": lax.rem(samp + k, SAMP)}, device_id_type=MESH,
        ).start()
        return 0

    lax.fori_loop(1, SAMP, send_fin, 0)
    seven = fin.at[pl.ds(0, 7 * 32)]
    pltpu.make_async_copy(seven, seven, ag_sem.at[1]).wait()
    for slot, tap in enumerate(TAP_ORDER):
        for h in (0, 1):
            w2_out[tap, :, LANES * h : LANES * (h + 1)] = fin[128 * h + 4 * slot : 128 * h + 4 * slot + 4, :]

    halo.wait_send()
    pltpu.make_async_copy(
        cstage.at[pl.ds(0, GRP - 1)], cstage.at[pl.ds(0, GRP - 1)], cot_sem.at[0]
    ).wait()
    cx.wait_send()
    for c in act_copy + z_copies:
        c.wait_send()
    for which in (0, 1):
        pltpu.make_async_copy(recv_buf[which], recv_buf[which], rs_sem.at[0, which]).wait()
    pltpu.make_async_copy(seven, seven, ag_sem.at[0]).wait()


def on_device(volumes, w_first, bias_first, w_second, cotangent):
    any_space = pl.BlockSpec(memory_space=pltpu.HBM)
    vmem = pl.BlockSpec(memory_space=pltpu.VMEM)
    dma = pltpu.SemaphoreType.DMA
    recv_a = pltpu.VMEM((GRP - 1, ROWS_A, LANES), BF16)
    recv_b = pltpu.VMEM((GRP - 1, ROWS_B, LANES), BF16)
    scratch = [
        pltpu.VMEM((5, CIN, 16, LANES), BF16),
        pltpu.VMEM((TAPS * CIN, CH), BF16),
        pltpu.VMEM((CH, TAPS * CIN), BF16),
        pltpu.VMEM((1, CH), F32),
        pltpu.VMEM((TAPS, FILT, CH), BF16),
        pltpu.VMEM((8, GRP, LANES), BF16),
        pltpu.VMEM((GRP * 16, LANES), F32),
        pltpu.VMEM((GRP, 16, LANES), BF16),
        pltpu.VMEM((GRP, 16, LANES), BF16),
        pltpu.VMEM((2, FILT, LANES), BF16),
        pltpu.VMEM((2, HALF, LANES), BF16),
        pltpu.VMEM((256, 256), BF16),
        pltpu.VMEM((5, 16, CIN, LANES), BF16),
        pltpu.VMEM((5, 4, CIN, LANES), BF16),
        pltpu.VMEM((5, 4, CIN, LANES), BF16),
        pltpu.VMEM((5, CIN, LANES), BF16),
        pltpu.VMEM((2, 4, CH, LANES), F32),
        pltpu.VMEM((2, 4, CH, LANES), BF16),
        pltpu.VMEM((2, 4, CH, LANES), BF16),
        pltpu.VMEM((2, CH, LANES), F32),
        pltpu.VMEM((GRP // 2, 2, ROWS, LANES), BF16),
        recv_a,
        recv_b,
        pltpu.VMEM((128, LANES), F32),
        pltpu.VMEM((3, 32, LANES), F32),
        pltpu.VMEM((2 * 128, LANES), F32),
        pltpu.VMEM((2, 4, LANES, FILT), BF16),
        pltpu.VMEM((CH * 8, LANES), F32),
        dma((4,)),
        dma((4,)),
        dma((2,)),
        dma((2,)),
        dma((2,)),
        dma((2, 2)),
        dma((2, 2)),
        dma((2, 3)),
        dma((2,)),
    ]

    def body(*refs):
        refs = list(refs)
        at = 7 + 20 + 1
        both = tuple(refs[at : at + 2])
        kernel(*refs[:at], both, *refs[at + 2 :])

    pre, w2g = pl.pallas_call(
        body,
        out_shape=(
            jax.ShapeDtypeStruct((CH, 8, LANES), BF16),
            jax.ShapeDtypeStruct((TAPS, 4, FILT), F32),
        ),
        in_specs=[any_space] * 5,
        out_specs=(vmem, vmem),
        scratch_shapes=scratch,
        compiler_params=pltpu.CompilerParams(
            collective_id=0, has_side_effects=True, vmem_limit_bytes=48 * 1024 * 1024
        ),
        name="layers",
    )(
        volumes[0],
        jnp.transpose(w_first),
        bias_first.reshape(1, CH),
        jnp.transpose(w_second, (1, 0, 2)),
        cotangent[0],
    )
    return pre.reshape(1, CH, 2, 4, LANES), jnp.transpose(w2g, (2, 0, 1))


def solution(mesh):
    placed = (P("samp", None, "grp", None, None), P(), P(), P(), P("samp", "grp", None, None))
    return jax.shard_map(
        on_device,
        mesh=mesh,
        in_specs=placed,
        out_specs=(P("samp", None, "grp", None, None), P(None, None, "grp")),
        check_vma=False,
    )
```

time: 313 us -> 51.6 us (0.16)
  waiting for transfers between devices: 128 us -> 0 us
  local copies, waits for them, and re-layouts: 122 us -> 6.55 us
  Pallas kernels: 0 us -> 44.1 us
  other arithmetic: 25.7 us -> 0 us
  between operations: 15.4 us -> 0.65 us
  starting transfers between devices: 12.8 us -> 0 us
  matrix products: 8.2 us -> 0 us
    psum x1 -> x0, waiting for transfers between devices: 90.8 us -> none  [on_device(): w2_grad = lax.psum(partial_grad, 'samp') * (1.0 / math.sqrt(total_cells))]
    pallas_call x0 -> x1, Pallas kernels: none -> 44.1 us  [on_device(): pl.pallas_call(body, out_shape=(jax.ShapeDtypeStruct((CH, 8, LANES), BF16...]
    unnamed x148 -> x12, local copies, waits for them, and re-layouts: 35.8 us -> 6.55 us
    concatenate x54 -> x0, local copies, waits for them, and re-layouts: 28.7 us -> none  [the longest x23 11.4 us: shift_cells(): jnp.roll(field, 1, axis=-1)]
    reshape x31 -> x0, local copies, waits for them, and re-layouts: 26.2 us -> none  [the longest x27 23.9 us: first_patches(): pieces.append(jnp.stack(phases, axis=2).reshape(channels, -1))]
    all_gather x1 -> x0, waiting for transfers between devices: 24.8 us -> none  [on_device(): lax.all_gather(cotangent[0], 'grp', axis=0, tiled=True).reshape(filters, -1)]
    another operation x28 -> x0, local copies, waits for them, and re-layouts: 13.2 us -> none  [the longest x27 13.2 us: first_patches(): pieces.append(jnp.stack(phases, axis=2).reshape(channels, -1))]
    slice x54 -> x0, local copies, waits for them, and re-layouts: 12.1 us -> none  [the longest x5 3.64 us: first_patches(): picked = plane_set[:, :, 4 * (along_y % 4) + along_z % 4]]
  transfers between devices with their start and end apart: 5 -> 0, of which waited for: 4 -> 0; matrix products, arithmetic and copies ran while one was open for 38% -> 0% of each run, Pallas kernels for 0% -> 0%
where the time goes in v1:
time: 51.6 us; the launch traced here: 51.3 us
  Pallas kernels  44.1 us (85%)
  local copies, waits for them, and re-layouts  6.55 us (13%)
  between operations  0.65 us (1%)
    pallas_call x1, Pallas kernels, on_device(): pl.pallas_call(body, out_shape=(jax.ShapeDtypeStruct((CH, 8, LANES), BF16...  44.1 us
    unnamed x12, local copies, waits for them, and re-layouts  6.55 us

profile of v1, /device:TPU:1, one launch (start us, length us, event | category | flops | bytes accessed | tf_op | source)
XLA Modules:
  0.0 51.3 jit_solution(5815537377949554488)
XLA Ops:
  0.6 0.0 copy-start
  0.6 1.5 %copy-done = bf16[256,27,128]{2,0,1:T(8,128)(2,1)S(1)} copy-done((bf16[256,27,128]{2,0,1:T(8,128)(2,1)S(1)}, bf16[256,27,128]{2,0,1:T(8,128)(2,1)}, u32[]{:S(2)}) %copy-start) | copy-done | bytes 1769496
  2.1 0.0 copy-start.1
  2.1 1.2 %copy-done.1 = bf16[1,64,4,16,128]{4,3,2,1,0:T(8,128)(2,1)S(1)} copy-done((bf16[1,64,4,16,128]{4,3,2,1,0:T(8,128)(2,1)S(1)}, bf16[1,64,4,16,128]{4,3,2,1,0:T(8,128)(2,1)}, u32[]{:S(2)}) %copy-start.1) | copy-done | bytes 1048600
  3.3 0.0 copy-start.2
  3.3 1.0 %copy-done.2 = bf16[128,1728]{0,1:T(8,128)(2,1)S(1)} copy-done((bf16[128,1728]{0,1:T(8,128)(2,1)S(1)}, bf16[128,1728]{0,1:T(8,128)(2,1)}, u32[]{:S(2)}) %copy-start.2) | copy-done | bytes 442392
  4.3 0.0 copy-start.3
  4.3 0.8 %copy-done.3 = bf16[1,8,32,128]{3,2,1,0:T(8,128)(2,1)S(1)} copy-done((bf16[1,8,32,128]{3,2,1,0:T(8,128)(2,1)S(1)}, bf16[1,8,32,128]{3,2,1,0:T(8,128)(2,1)}, u32[]{:S(2)}) %copy-start.3) | copy-done | bytes 65560
  5.2 0.0 copy-start.4
  5.2 0.7 %copy-done.4 = f32[128]{0:T(128)S(1)} copy-done((f32[128]{0:T(128)S(1)}, f32[128]{0:T(128)}, u32[]{:S(2)}) %copy-start.4) | copy-done | bytes 536
  5.8 44.1 %layers.1 = (bf16[128,8,128]{2,1,0:T(8,128)(2,1)S(1)}, f32[27,4,256]{2,1,0:T(4,128)S(1)}) custom-call(bf16[64,4,16,128]{3,2,1,0:T(8,128)(2,1)S(1)} %bitcast.8, bf16[1728,128]{1,0:T(8,128)(2,1)S(1)} %bitcast.9, f32[1,128]{1,0:T(1,128)S(1)} %bitcast.13, bf16[27,256,128]{2,1,0:T(8,128)(2,1)S(1)} %bitcast.7, bf16[8,32,128]{2,1,0:T(8,128)(2,1)S(1)} %bitcast.12), custom_call_target="tpu_custom_call" | custom-call | tf_op jit(solution)/shard_map/layers/pallas_call | solution.py:426
  50.0 0.7 %copy.9 = bf16[1,128,2,4,128]{4,3,2,1,0:T(4,128)(2,1)} copy(bf16[1,128,2,4,128]{4,3,2,1,0:T(4,128)(2,1)S(1)} %bitcast.10) | data formatting | bytes 524288
  50.7 0.6 %copy.10 = f32[256,27,4]{0,2,1:T(4,128)} copy(f32[256,27,4]{0,2,1:T(4,128)S(1)} %bitcast.11) | data formatting | bytes 221184
Async XLA Ops:
  0.6 1.5 %copy-start = (bf16[256,27,128]{2,0,1:T(8,128)(2,1)S(1)}, bf16[256,27,128]{2,0,1:T(8,128)(2,1)}, u32[]{:S(2)}) copy-start(bf16[256,27,128]{2,0,1:T(8,128)(2,1)} %param.8) | copy-start | bytes 5308420
  2.1 1.2 %copy-start.1 = (bf16[1,64,4,16,128]{4,3,2,1,0:T(8,128)(2,1)S(1)}, bf16[1,64,4,16,128]{4,3,2,1,0:T(8,128)(2,1)}, u32[]{:S(2)}) copy-start(bf16[1,64,4,16,128]{4,3,2,1,0:T(8,128)(2,1)} %param.5) | copy-start | bytes 3145732
  3.3 1.0 %copy-start.2 = (bf16[128,1728]{0,1:T(8,128)(2,1)S(1)}, bf16[128,1728]{0,1:T(8,128)(2,1)}, u32[]{:S(2)}) copy-start(bf16[128,1728]{0,1:T(8,128)(2,1)} %param.6) | copy-start | bytes 1327108
  4.3 0.8 %copy-start.3 = (bf16[1,8,32,128]{3,2,1,0:T(8,128)(2,1)S(1)}, bf16[1,8,32,128]{3,2,1,0:T(8,128)(2,1)}, u32[]{:S(2)}) copy-start(bf16[1,8,32,128]{3,2,1,0:T(8,128)(2,1)} %param.9) | copy-start | bytes 196612
  5.2 0.7 %copy-start.4 = (f32[128]{0:T(128)S(1)}, f32[128]{0:T(128)}, u32[]{:S(2)}) copy-start(f32[128]{0:T(128)} %param.7) | copy-start | bytes 1540

commit v2 on v1

--- a/solution.py
+++ b/solution.py
@@ -1,4 +1,3 @@
-import functools
 import math
 
 import jax
@@ -28,6 +27,8 @@
 ROWS_A = 64
 ROWS_B = 48
 ROWS = ROWS_A + ROWS_B
+K_BACK = 9 * CIN
+SCALE = 1.0 / math.sqrt(32768)
 
 
 def lane_index(shape):
@@ -56,26 +57,27 @@
 def kernel(
     vol, w1t, bias, w2, cot,
     pre_out, w2_out,
-    vbuf, w1tv, w1s, biasv, w2v, cotv, cstg, cstage, crecv, cotf, cpart,
-    perm, tn, ty, tz, tyz, pre_s, act_own, act_part, carry, send_buf, recv_buf,
-    acc_s, zrecv, fin, cvar, pgf,
-    lsem, vsem, halo_sem, cot_sem, cx_sem, act_sem, rs_sem, z_sem, ag_sem,
+    vbuf, w1tv, w1_back, w1_rest, biasv, w2v, cotv, cstg, cstage, crecv, cotf, cpart,
+    perm, tn, ty, tz, tyz, hsend, hrecv, pre_s, act_own, act_part, carry, cvar, pgf,
+    send_buf, recv_a, recv_b, part_a, part_b,
+    lsem, vsem, halo_sem, cot_sem, cx_sem, act_sem, rs_sem, samp_sem,
 ):
+    recv_buf = (recv_a, recv_b)
+    part_buf = (part_a, part_b)
     me = lax.axis_index("grp")
     samp = lax.axis_index("samp")
     core = lax.rem(samp, 2)
-    zhi = lax.div(samp, 2)
     other = samp + 1 - 2 * core
 
     ld_cot = pltpu.make_async_copy(cot, cotv, lsem.at[0])
     ld_w1 = pltpu.make_async_copy(w1t, w1tv, lsem.at[1])
     ld_bias = pltpu.make_async_copy(bias, biasv, lsem.at[2])
     ld_w2 = pltpu.make_async_copy(w2, w2v, lsem.at[3])
-    ld_vol = [pltpu.make_async_copy(vol.at[:, x], vbuf.at[x + 1], vsem.at[x]) for x in range(4)]
+    ld_vol = [pltpu.make_async_copy(vol.at[:, x], vbuf.at[x], vsem.at[x]) for x in range(4)]
     ld_cot.start()
     ld_w1.start()
     ld_bias.start()
-    for x in (1, 2, 3, 0):
+    for x in (3, 1, 2, 0):
         ld_vol[x].start()
     ld_w2.start()
 
@@ -93,8 +95,8 @@
         )
         return 0
 
+    lax.fori_loop(1, SAMP, greet_samp, 0)
     lax.fori_loop(1, GRP, greet_grp, 0)
-    lax.fori_loop(1, SAMP, greet_samp, 0)
 
     ld_cot.wait()
     for f in range(8):
@@ -106,7 +108,7 @@
     pl.semaphore_wait(barrier, GRP - 1 + SAMP - 1)
 
     halo = pltpu.make_async_remote_copy(
-        src_ref=vol.at[:, 3], dst_ref=vbuf.at[0],
+        src_ref=hsend, dst_ref=hrecv,
         send_sem=halo_sem.at[0], recv_sem=halo_sem.at[1],
         device_id={"grp": lax.rem(me + 1, GRP)}, device_id_type=MESH,
     )
@@ -121,12 +123,12 @@
         return 0
 
     lax.fori_loop(1, GRP, send_cot, 0)
-    halo.start()
     crecv[me] = cstage[me]
 
     ld_w1.wait()
     ld_bias.wait()
-    w1s[...] = jnp.transpose(w1tv[...])
+    w1_back[...] = jnp.transpose(w1tv[:K_BACK, :])
+    w1_rest[...] = jnp.transpose(w1tv[K_BACK:, :])
     bias_rows = jnp.transpose(jnp.broadcast_to(biasv[...], (CH, CH)))
     row = lax.broadcasted_iota(jnp.int32, (256, 256), 0)
     col = lax.broadcasted_iota(jnp.int32, (256, 256), 1)
@@ -155,22 +157,20 @@
             return tz[x, ry]
         return tn[x, 4 * ry + rz]
 
-    def first_layer(i):
-        for pair in (0, 1):
-            columns = []
-            for q in (2 * pair, 2 * pair + 1):
-                qy, qz = PHASES[q]
-                columns.append(
-                    jnp.concatenate(
-                        [patch(2 * i + a, qy, qz, b, e) for a in range(3) for b, e in COMBOS], axis=0
-                    )
-                )
-            patches = jnp.concatenate(columns, axis=1)
-            pre = jnp.dot(w1s[...], patches, preferred_element_type=F32)
-            for h in (0, 1):
-                part = pre[:, LANES * h : LANES * (h + 1)] + bias_rows
-                pre_s[i, 2 * pair + h] = part
-                act_own[i, 2 * pair + h] = (part / (1.0 + jnp.exp(-part))).astype(BF16)
+    def products(weights, planes, pair):
+        columns = []
+        for q in (2 * pair, 2 * pair + 1):
+            qy, qz = PHASES[q]
+            columns.append(
+                jnp.concatenate([patch(x, qy, qz, b, e) for x in planes for b, e in COMBOS], axis=0)
+            )
+        return jnp.dot(
+            weights[...], jnp.concatenate(columns, axis=1), preferred_element_type=F32
+        )
+
+    def activate(i, q, z):
+        pre_s[i, q] = z
+        act_own[i, q] = (z / (1.0 + jnp.exp(-z))).astype(BF16)
 
     def exchange_act(i):
         return pltpu.make_async_remote_copy(
@@ -179,12 +179,30 @@
             device_id={"samp": other}, device_id_type=MESH,
         )
 
-    for x in (1, 2, 3):
+    ld_vol[3].wait()
+    by_phase(3)
+    for pair in (0, 1):
+        back = products(w1_back, (3,), pair).astype(BF16)
+        hsend[2 * pair] = back[:, :LANES]
+        hsend[2 * pair + 1] = back[:, LANES:]
+    halo.start()
+
+    for x in (1, 2):
         ld_vol[x].wait()
-        by_phase(x + 1)
-    first_layer(1)
+        by_phase(x)
+    for pair in (0, 1):
+        pre = products(w1_back, (1,), pair) + products(w1_rest, (2, 3), pair)
+        for h in (0, 1):
+            activate(1, 2 * pair + h, pre[:, LANES * h : LANES * (h + 1)] + bias_rows)
     act_copy = [exchange_act(0), exchange_act(1)]
     act_copy[1].start()
+
+    ld_vol[0].wait()
+    by_phase(0)
+    for pair in (0, 1):
+        pre = products(w1_rest, (0, 1), pair)
+        for h in (0, 1):
+            pre_s[0, 2 * pair + h] = pre[:, LANES * h : LANES * (h + 1)] + bias_rows
 
     pltpu.make_async_copy(
         crecv.at[pl.ds(0, GRP - 1)], crecv.at[pl.ds(0, GRP - 1)], cot_sem.at[1]
@@ -198,9 +216,6 @@
         device_id={"samp": other}, device_id_type=MESH,
     )
     cx.start()
-
-    ld_vol[0].wait()
-    by_phase(1)
 
     my_half = pl.ds(pl.multiple_of(HALF * core, HALF), HALF)
 
@@ -265,8 +280,8 @@
     send_chunk(0)
 
     halo.wait_recv()
-    by_phase(0)
-    first_layer(0)
+    for q in range(4):
+        activate(0, q, pre_s[0, q] + hrecv[q].astype(F32))
     act_copy[0].start()
 
     for p in (0, 1):
@@ -313,74 +328,62 @@
     pre_out[...] = pgf[...].reshape(CH, 8, LANES).astype(BF16)
 
     mine = send_buf.at[lax.div(me, 2), lax.rem(me, 2)]
-    for which, rows in ((0, pl.ds(0, ROWS_A)), (1, pl.ds(ROWS_A, ROWS_B))):
-        pltpu.make_async_copy(recv_buf[which], recv_buf[which], rs_sem.at[1, which]).wait()
-        acc_s[rows, :] = lax.fori_loop(
+    chunk_rows = (pl.ds(0, ROWS_A), pl.ds(ROWS_A, ROWS_B))
+    for which in (0, 1):
+        received, parts = recv_buf[which], part_buf[which]
+        pltpu.make_async_copy(received, received, rs_sem.at[1, which]).wait()
+        parts[samp] = lax.fori_loop(
             0,
             GRP - 1,
-            lambda j, acc: acc + recv_buf[which][j].astype(F32),
-            mine[rows, :].astype(F32),
-        )
-    acc_s[pl.ds(ROWS, 128 - ROWS), :] = jnp.zeros((128 - ROWS, LANES), F32)
-
-    def z_peer(k):
-        return lax.rem(zhi + k, 4)
-
-    z_copies = []
-    for k in (1, 2, 3):
-        peer = z_peer(k)
-        z_copies.append(
+            lambda j, acc, received=received: acc + received[j].astype(F32),
+            mine[chunk_rows[which], :].astype(F32),
+        ).astype(BF16)
+
+        def send_part(k, _, parts=parts, which=which):
             pltpu.make_async_remote_copy(
-                src_ref=acc_s.at[pl.ds(pl.multiple_of(32 * peer, 32), 32)], dst_ref=zrecv.at[k - 1],
-                send_sem=z_sem.at[0, k - 1], recv_sem=z_sem.at[1, k - 1],
-                device_id={"samp": 2 * peer + core}, device_id_type=MESH,
-            )
-        )
-        z_copies[-1].start()
-    for c in z_copies:
-        c.wait_recv()
-    scale = 1.0 / math.sqrt(32768)
-    my_rows = pl.ds(pl.multiple_of(32 * zhi, 32), 32)
-    fin_rows = pl.ds(pl.multiple_of(128 * core + 32 * zhi, 32), 32)
-    fin[fin_rows, :] = (acc_s[my_rows, :] + zrecv[0] + zrecv[1] + zrecv[2]) * scale
-
-    def send_fin(k, _):
-        pltpu.make_async_remote_copy(
-            src_ref=fin.at[fin_rows], dst_ref=fin.at[fin_rows],
-            send_sem=ag_sem.at[0], recv_sem=ag_sem.at[1],
-            device_id={"samp": lax.rem(samp + k, SAMP)}, device_id_type=MESH,
-        ).start()
-        return 0
-
-    lax.fori_loop(1, SAMP, send_fin, 0)
-    seven = fin.at[pl.ds(0, 7 * 32)]
-    pltpu.make_async_copy(seven, seven, ag_sem.at[1]).wait()
-    for slot, tap in enumerate(TAP_ORDER):
+                src_ref=parts.at[samp], dst_ref=parts.at[samp],
+                send_sem=samp_sem.at[0, which], recv_sem=samp_sem.at[1, which],
+                device_id={"samp": lax.rem(samp + k, SAMP)}, device_id_type=MESH,
+            ).start()
+            return 0
+
+        lax.fori_loop(1, SAMP, send_part, 0)
+
+    for which in (0, 1):
+        parts = part_buf[which]
+        seven = parts.at[pl.ds(0, SAMP - 1)]
+        pltpu.make_async_copy(seven, seven, samp_sem.at[1, which]).wait()
         for h in (0, 1):
-            w2_out[tap, :, LANES * h : LANES * (h + 1)] = fin[128 * h + 4 * slot : 128 * h + 4 * slot + 4, :]
+            total = sum(parts[h + 2 * j].astype(F32) for j in range(SAMP // 2)) * SCALE
+            first = 0 if which == 0 else ROWS_A // 4
+            for slot in range(total.shape[0] // 4):
+                if first + slot < TAPS:
+                    w2_out[TAP_ORDER[first + slot], :, LANES * h : LANES * (h + 1)] = total[
+                        4 * slot : 4 * slot + 4
+                    ]
 
     halo.wait_send()
     pltpu.make_async_copy(
         cstage.at[pl.ds(0, GRP - 1)], cstage.at[pl.ds(0, GRP - 1)], cot_sem.at[0]
     ).wait()
     cx.wait_send()
-    for c in act_copy + z_copies:
+    for c in act_copy:
         c.wait_send()
     for which in (0, 1):
         pltpu.make_async_copy(recv_buf[which], recv_buf[which], rs_sem.at[0, which]).wait()
-    pltpu.make_async_copy(seven, seven, ag_sem.at[0]).wait()
+        seven = part_buf[which].at[pl.ds(0, SAMP - 1)]
+        pltpu.make_async_copy(seven, seven, samp_sem.at[0, which]).wait()
 
 
 def on_device(volumes, w_first, bias_first, w_second, cotangent):
     any_space = pl.BlockSpec(memory_space=pltpu.HBM)
     vmem = pl.BlockSpec(memory_space=pltpu.VMEM)
     dma = pltpu.SemaphoreType.DMA
-    recv_a = pltpu.VMEM((GRP - 1, ROWS_A, LANES), BF16)
-    recv_b = pltpu.VMEM((GRP - 1, ROWS_B, LANES), BF16)
     scratch = [
-        pltpu.VMEM((5, CIN, 16, LANES), BF16),
+        pltpu.VMEM((4, CIN, 16, LANES), BF16),
         pltpu.VMEM((TAPS * CIN, CH), BF16),
-        pltpu.VMEM((CH, TAPS * CIN), BF16),
+        pltpu.VMEM((CH, K_BACK), BF16),
+        pltpu.VMEM((CH, TAPS * CIN - K_BACK), BF16),
         pltpu.VMEM((1, CH), F32),
         pltpu.VMEM((TAPS, FILT, CH), BF16),
         pltpu.VMEM((8, GRP, LANES), BF16),
@@ -390,22 +393,23 @@
         pltpu.VMEM((2, FILT, LANES), BF16),
         pltpu.VMEM((2, HALF, LANES), BF16),
         pltpu.VMEM((256, 256), BF16),
-        pltpu.VMEM((5, 16, CIN, LANES), BF16),
-        pltpu.VMEM((5, 4, CIN, LANES), BF16),
-        pltpu.VMEM((5, 4, CIN, LANES), BF16),
-        pltpu.VMEM((5, CIN, LANES), BF16),
+        pltpu.VMEM((4, 16, CIN, LANES), BF16),
+        pltpu.VMEM((4, 4, CIN, LANES), BF16),
+        pltpu.VMEM((4, 4, CIN, LANES), BF16),
+        pltpu.VMEM((4, CIN, LANES), BF16),
+        pltpu.VMEM((4, CH, LANES), BF16),
+        pltpu.VMEM((4, CH, LANES), BF16),
         pltpu.VMEM((2, 4, CH, LANES), F32),
         pltpu.VMEM((2, 4, CH, LANES), BF16),
         pltpu.VMEM((2, 4, CH, LANES), BF16),
         pltpu.VMEM((2, CH, LANES), F32),
-        pltpu.VMEM((GRP // 2, 2, ROWS, LANES), BF16),
-        recv_a,
-        recv_b,
-        pltpu.VMEM((128, LANES), F32),
-        pltpu.VMEM((3, 32, LANES), F32),
-        pltpu.VMEM((2 * 128, LANES), F32),
         pltpu.VMEM((2, 4, LANES, FILT), BF16),
         pltpu.VMEM((CH * 8, LANES), F32),
+        pltpu.VMEM((GRP // 2, 2, ROWS, LANES), BF16),
+        pltpu.VMEM((GRP - 1, ROWS_A, LANES), BF16),
+        pltpu.VMEM((GRP - 1, ROWS_B, LANES), BF16),
+        pltpu.VMEM((SAMP, ROWS_A, LANES), BF16),
+        pltpu.VMEM((SAMP, ROWS_B, LANES), BF16),
         dma((4,)),
         dma((4,)),
         dma((2,)),
@@ -413,18 +417,11 @@
         dma((2,)),
         dma((2, 2)),
         dma((2, 2)),
-        dma((2, 3)),
-        dma((2,)),
+        dma((2, 2)),
     ]
 
-    def body(*refs):
-        refs = list(refs)
-        at = 7 + 20 + 1
-        both = tuple(refs[at : at + 2])
-        kernel(*refs[:at], both, *refs[at + 2 :])
-
     pre, w2g = pl.pallas_call(
-        body,
+        kernel,
         out_shape=(
             jax.ShapeDtypeStruct((CH, 8, LANES), BF16),
             jax.ShapeDtypeStruct((TAPS, 4, FILT), F32),
@@ -433,7 +430,7 @@
         out_specs=(vmem, vmem),
         scratch_shapes=scratch,
         compiler_params=pltpu.CompilerParams(
-            collective_id=0, has_side_effects=True, vmem_limit_bytes=48 * 1024 * 1024
+            collective_id=0, has_side_effects=True, vmem_limit_bytes=60 * 1024 * 1024
         ),
         name="layers",
     )(

time: 51.6 us -> 42.8 us (0.83)
  Pallas kernels: 44.1 us -> 38.7 us
  local copies, waits for them, and re-layouts: 6.55 us -> 3.29 us
    pallas_call x1, Pallas kernels: 44.1 us -> 38.7 us  [on_device(): pl.pallas_call(kernel, out_shape=(jax.ShapeDtypeStruct((CH, 8, LANES), BF...]
    unnamed x12 -> x2, local copies, waits for them, and re-layouts: 6.55 us -> 3.29 us
where the time goes in v2:
time: 42.8 us; the launch traced here: 42.6 us
  Pallas kernels  38.7 us (90%)
  local copies, waits for them, and re-layouts  3.29 us (8%)
  between operations  0.64 us (1%)
    pallas_call x1, Pallas kernels, on_device(): pl.pallas_call(kernel, out_shape=(jax.ShapeDtypeStruct((CH, 8, LANES), BF...  38.7 us
    unnamed x2, local copies, waits for them, and re-layouts  3.29 us

profile of v2, /device:TPU:1, one launch (start us, length us, event | category | flops | bytes accessed | tf_op | source)
XLA Modules:
  0.0 42.6 jit_solution(1250409714296487433)
XLA Ops:
  0.6 38.7 %layers.1 = (bf16[128,8,128]{2,1,0:T(8,128)(2,1)}, f32[27,4,256]{2,1,0:T(4,128)}) custom-call(bf16[64,4,16,128]{3,2,1,0:T(8,128)(2,1)} %bitcast.8, bf16[1728,128]{1,0:T(8,128)(2,1)} %bitcast.9, f32[1,128]{1,0:T(1,128)} %bitcast.13, bf16[27,256,128]{2,1,0:T(8,128)(2,1)} %bitcast.7, bf16[8,32,128]{2,1,0:T(8,128)(2,1)} %bitcast.12), custom_call_target="tpu_custom_call" | custom-call | tf_op jit(solution)/shard_map/layers/pallas_call | solution.py:423
  39.4 1.7 %copy.9 = bf16[1,128,2,4,128]{4,3,2,1,0:T(4,128)(2,1)} copy(bf16[1,128,2,4,128]{4,3,2,1,0:T(4,128)(2,1)} %bitcast.10) | data formatting | bytes 524288
  41.1 1.5 %copy.10 = f32[256,27,4]{0,2,1:T(4,128)} copy(f32[256,27,4]{0,2,1:T(4,128)} %bitcast.11) | data formatting | bytes 221184

commit v3 on v2

v3 whole, which is shorter than its diff:
```python
import math

import jax
import jax.numpy as jnp
from jax import lax
from jax.experimental import pallas as pl
from jax.experimental.pallas import tpu as pltpu
from jax.sharding import PartitionSpec as P

MESH = pl.DeviceIdType.MESH
F32 = jnp.float32
BF16 = jnp.bfloat16

CIN = 64
CH = 128
FILT = 256
LANES = 128
ZQ = 16
GRP = 32
SAMP = 8
TAPS = 27
COMBOS = [(b, e) for b in (-1, 0, 1) for e in (-1, 0, 1)]
PHASES = [(0, 0), (0, 1), (1, 0), (1, 1)]
QUARTER = 32
ROWS = 32
CHUNK_TAPS = (((0, 8), (18, 8)), ((8, 10), (26, 1)))
CHUNK_HALF = (16, 12)
OUT_ROWS = 112
K_BACK = 9 * CIN
SCALE = 1.0 / math.sqrt(32768)


def lane_index(shape):
    return lax.broadcasted_iota(jnp.int32, shape, len(shape) - 1)


def y_before(x):
    return pltpu.roll(x, ZQ, 1)


def z_before(x):
    first = lane_index(x.shape) % ZQ == 0
    return jnp.where(first, pltpu.roll(x, LANES + 1 - ZQ, 1), pltpu.roll(x, 1, 1))


def row_y_after(x):
    return jnp.concatenate([x[ZQ:], x[:ZQ]], axis=0)


def row_z_after(x):
    rows = x.shape[0]
    last = lax.broadcasted_iota(jnp.int32, x.shape, 0) % ZQ == ZQ - 1
    return jnp.where(last, pltpu.roll(x, ZQ - 1, 0), pltpu.roll(x, rows - 1, 0))


def kernel(
    vol, w1t, bias, w2, cot,
    pre_out, w2_out,
    vbuf, w1tv, w1_back, w1_rest, biasv, w2v, cotv, cot_32, cstg, cstage, crecv, cots,
    perm, tn, ty, tz, tyz, hsend, hrecv, pre_s, act_32, act_own, act_in, cvar, pgf,
    stage, send_buf, recv_a, recv_b, part_a, part_b, fin,
    lsem, vsem, halo_sem, cot_sem, cx_sem, act_sem, rs_sem, samp_sem,
):
    recv_buf = (recv_a, recv_b)
    part_buf = (part_a, part_b)
    me = lax.axis_index("grp")
    samp = lax.axis_index("samp")
    core = lax.rem(samp, 2)
    other = samp + 1 - 2 * core
    odd = lax.rem(me, 2)
    quarter = 2 * core + odd

    ld_cot = pltpu.make_async_copy(cot, cotv, lsem.at[0])
    ld_w1 = pltpu.make_async_copy(w1t, w1tv, lsem.at[1])
    ld_bias = pltpu.make_async_copy(bias, biasv, lsem.at[2])
    ld_w2 = pltpu.make_async_copy(w2, w2v, lsem.at[3])
    ld_vol = [pltpu.make_async_copy(vol.at[:, x], vbuf.at[x], vsem.at[x]) for x in range(4)]
    ld_cot.start()
    ld_w1.start()
    ld_bias.start()
    for x in (3, 1, 2, 0):
        ld_vol[x].start()
    ld_w2.start()

    barrier = pltpu.get_barrier_semaphore()

    def greet_grp(k, _):
        pl.semaphore_signal(
            barrier, inc=1, device_id={"grp": lax.rem(me + k, GRP)}, device_id_type=MESH
        )
        return 0

    def greet_samp(k, _):
        pl.semaphore_signal(
            barrier, inc=1, device_id={"samp": lax.rem(samp + k, SAMP)}, device_id_type=MESH
        )
        return 0

    lax.fori_loop(1, SAMP, greet_samp, 0)
    lax.fori_loop(1, GRP, greet_grp, 0)
    pl.semaphore_signal(
        barrier, inc=1, device_id={"samp": other, "grp": me + 1 - 2 * odd}, device_id_type=MESH
    )

    ld_cot.wait()
    for f in range(8):
        x = cotv[f].astype(F32)
        cot_32[40 * f : 40 * f + GRP, :] = x
        cot_32[40 * f + GRP : 40 * f + 40, :] = x[:8]
    for f in range(8):
        for p in range(4):
            cstg[pl.ds(8 * p + f, GRP // 2, stride=32), :] = cot_32[
                pl.ds(40 * f + p, GRP // 2, stride=2), :
            ]
    cstage[...] = cstg[...].reshape(GRP // 2, 32, LANES).astype(BF16)

    ld_w1.wait()
    ld_bias.wait()
    w1_back[...] = jnp.transpose(w1tv[:K_BACK, :])
    w1_rest[...] = jnp.transpose(w1tv[K_BACK:, :])
    bias_rows = jnp.transpose(jnp.broadcast_to(biasv[...], (CH, CH)))
    row = lax.broadcasted_iota(jnp.int32, (256, 256), 0)
    col = lax.broadcasted_iota(jnp.int32, (256, 256), 1)
    perm[...] = jnp.where(col == (row % 16) * 16 + row // 16, 1.0, 0.0).astype(BF16)

    def by_phase(x):
        for blk in range(4):
            rows = vbuf[x, 16 * blk : 16 * blk + 16].reshape(256, LANES)
            moved = jnp.dot(perm[...], rows, preferred_element_type=F32)
            here = slice(16 * blk, 16 * blk + 16)
            tn[x, :, here, :] = moved.reshape(16, 16, LANES).astype(BF16)
            ty[x, :, here, :] = y_before(moved[192:256]).reshape(4, 16, LANES).astype(BF16)
            ends = jnp.concatenate([moved[64 * r + 48 : 64 * r + 64] for r in range(4)], axis=0)
            ends = z_before(ends)
            tz[x, :, here, :] = ends.reshape(4, 16, LANES).astype(BF16)
            tyz[x, here, :] = y_before(ends[48:64]).astype(BF16)

    def patch(x, qy, qz, b, e):
        along_y, along_z = 2 * qy + b, 2 * qz + e
        ry, rz = along_y % 4, along_z % 4
        if along_y < 0 and along_z < 0:
            return tyz[x]
        if along_y < 0:
            return ty[x, rz]
        if along_z < 0:
            return tz[x, ry]
        return tn[x, 4 * ry + rz]

    def products(weights, planes, pair):
        columns = []
        for q in (2 * pair, 2 * pair + 1):
            qy, qz = PHASES[q]
            columns.append(
                jnp.concatenate([patch(x, qy, qz, b, e) for x in planes for b, e in COMBOS], axis=0)
            )
        return jnp.dot(
            weights[...], jnp.concatenate(columns, axis=1), preferred_element_type=F32
        )

    def activate(i, q, z):
        pre_s[i, q] = z
        act_32[...] = z / (1.0 + jnp.exp(-z))
        for r in range(4):
            act_own[i, r, q] = act_32[pl.ds(r, QUARTER, stride=4), :].astype(BF16)

    def send_act(i):
        def body(k, _):
            to = lax.rem(quarter + k, 4)
            pltpu.make_async_remote_copy(
                src_ref=act_own.at[i, to], dst_ref=act_in.at[i, quarter],
                send_sem=act_sem.at[0, i], recv_sem=act_sem.at[1, i],
                device_id={
                    "samp": samp - core + lax.div(to, 2),
                    "grp": me - odd + lax.rem(to, 2),
                },
                device_id_type=MESH,
            ).start()
            return 0

        lax.fori_loop(1, 4, body, 0)
        act_in[i, quarter] = act_own[i, quarter]

    def wait_act(i, end):
        three = act_in.at[i, pl.ds(0, 3)]
        pltpu.make_async_copy(three, three, act_sem.at[end, i]).wait()

    ld_vol[3].wait()
    by_phase(3)
    for pair in (0, 1):
        back = products(w1_back, (3,), pair).astype(BF16)
        hsend[2 * pair] = back[:, :LANES]
        hsend[2 * pair + 1] = back[:, LANES:]
    stage[...] = jnp.zeros_like(stage)

    pl.semaphore_wait(barrier, GRP - 1 + SAMP - 1 + 1)

    halo = pltpu.make_async_remote_copy(
        src_ref=hsend, dst_ref=hrecv,
        send_sem=halo_sem.at[0], recv_sem=halo_sem.at[1],
        device_id={"grp": lax.rem(me + 1, GRP)}, device_id_type=MESH,
    )

    def send_cot(k, _):
        dest = lax.rem(me + k, GRP)
        pltpu.make_async_remote_copy(
            src_ref=cstage.at[lax.div(dest, 2)], dst_ref=crecv.at[me],
            send_sem=cot_sem.at[0], recv_sem=cot_sem.at[1],
            device_id={"grp": dest}, device_id_type=MESH,
        ).start()
        return 0

    lax.fori_loop(1, GRP, send_cot, 0)
    crecv[me] = cstage[lax.div(me, 2)]
    halo.start()

    for x in (1, 2):
        ld_vol[x].wait()
        by_phase(x)
    for pair in (0, 1):
        pre = products(w1_back, (1,), pair) + products(w1_rest, (2, 3), pair)
        for h in (0, 1):
            activate(1, 2 * pair + h, pre[:, LANES * h : LANES * (h + 1)] + bias_rows)
    send_act(1)

    ld_vol[0].wait()
    by_phase(0)
    for pair in (0, 1):
        pre = products(w1_rest, (0, 1), pair)
        for h in (0, 1):
            pre_s[0, 2 * pair + h] = pre[:, LANES * h : LANES * (h + 1)] + bias_rows

    pltpu.make_async_copy(
        crecv.at[pl.ds(0, GRP - 1)], crecv.at[pl.ds(0, GRP - 1)], cot_sem.at[1]
    ).wait()
    got = crecv[...].astype(F32)
    for p in range(3):
        cots[core, p] = got[:, 8 * p : 8 * p + 8].reshape(FILT, LANES).astype(BF16)
    cx = pltpu.make_async_remote_copy(
        src_ref=cots.at[core], dst_ref=cots.at[core],
        send_sem=cx_sem.at[0], recv_sem=cx_sem.at[1],
        device_id={"samp": other}, device_id_type=MESH,
    )
    cx.start()

    def second_patch(i, n):
        b, e = COMBOS[n]
        x = act_in[i, :, 2 * (b != 0) + (e != 0)].reshape(4 * QUARTER, LANES)
        if b < 0 or e < 0:
            x = x.astype(F32)
            if e < 0:
                x = z_before(x)
            if b < 0:
                x = y_before(x)
            x = x.astype(BF16)
        return jnp.concatenate([x[QUARTER * j : QUARTER * (j + 1)] for j in range(4)], axis=1)

    def filter_products(i, steps):
        left = jnp.concatenate([second_patch(i, n) for n in range(9)], axis=0)
        right = [
            jnp.concatenate([cots[j // 2, j % 2 + step] for j in range(4)], axis=1)
            for step in steps
        ]
        return lax.dot_general(
            left,
            jnp.concatenate(right, axis=0),
            (((1,), (1,)), ((), ())),
            preferred_element_type=F32,
        )

    def place(tap, rows):
        for which in (0, 1):
            at = 0
            for first, count in CHUNK_TAPS[which]:
                if first <= tap < first + count:
                    for h in (0, 1):
                        row = ROWS * which + CHUNK_HALF[which] * h + at + tap - first
                        stage[pl.ds(row, GRP, stride=2 * ROWS), :] = rows[
                            :, LANES * h : LANES * (h + 1)
                        ]
                at += count

    def send_chunk(which):
        staged = stage[...].reshape(GRP, 2 * ROWS, LANES)[:, ROWS * which : ROWS * (which + 1)]
        send_buf[which] = staged.astype(BF16)
        recv_buf[which][me] = send_buf[which, me]

        def body(k, _):
            dest = lax.rem(me + k, GRP)
            pltpu.make_async_remote_copy(
                src_ref=send_buf.at[which, dest], dst_ref=recv_buf[which].at[me],
                send_sem=rs_sem.at[0, which], recv_sem=rs_sem.at[1, which],
                device_id={"grp": dest}, device_id_type=MESH,
            ).start()
            return 0

        lax.fori_loop(1, GRP, body, 0)

    wait_act(1, 1)
    cx.wait_recv()
    grads = filter_products(1, (0, 1))
    for n in range(9):
        rows = grads[QUARTER * n : QUARTER * (n + 1)]
        place(18 + n, rows[:, :FILT])
        place(n, rows[:, FILT:])
    send_chunk(0)

    halo.wait_recv()
    for q in range(4):
        activate(0, q, pre_s[0, q] + hrecv[q].astype(F32))
    send_act(0)

    for p in (0, 1):
        turned = jnp.transpose(cots[core, odd + p].astype(F32))
        cvar[p, 0] = turned.astype(BF16)
        cvar[p, 2] = row_y_after(turned).astype(BF16)
        after = row_z_after(turned)
        cvar[p, 1] = after.astype(BF16)
        cvar[p, 3] = row_y_after(after).astype(BF16)

    wait_act(0, 1)
    grads = filter_products(0, (0,))
    for n in range(9):
        place(9 + n, grads[QUARTER * n : QUARTER * (n + 1)])
    send_chunk(1)

    ld_w2.wait()
    for i in (0, 1):
        for q, (qy, qz) in enumerate(PHASES):
            left, right = [], []
            for a, p in ((0, 0),) if i == 0 else ((1, 0), (-1, 1)):
                for b, sy in ((0, 0),) if qy == 0 else ((1, 0), (-1, 1)):
                    for e, sz in ((0, 0),) if qz == 0 else ((1, 0), (-1, 1)):
                        left.append(cvar[p, 2 * sy + sz])
                        right.append(w2v[9 * (a + 1) + 3 * (b + 1) + e + 1])
            grad = jnp.dot(
                jnp.concatenate(left, axis=1),
                jnp.concatenate(right, axis=0),
                preferred_element_type=F32,
            )
            grad = jnp.transpose(grad.astype(BF16).astype(F32))
            z = pre_s[i, q]
            g = 1.0 / (1.0 + jnp.exp(-z))
            pgf[pl.ds(4 * i + q, CH, stride=8), :] = grad * (g * (1.0 + z * (1.0 - g)))
    pre_out[...] = pgf[...].reshape(CH, 8, LANES).astype(BF16)

    most = pl.ds(0, GRP - 1)
    for which in (0, 1):
        received, parts = recv_buf[which], part_buf[which]
        pltpu.make_async_copy(received.at[most], received.at[most], rs_sem.at[1, which]).wait()
        total = lax.fori_loop(
            0,
            GRP // 2,
            lambda j, acc, received=received: acc + received[pl.ds(2 * j, 2)].astype(F32),
            jnp.zeros((2, ROWS, LANES), F32),
        )
        used = 2 * CHUNK_HALF[which]
        parts[samp] = total[:, :used].reshape(2 * used, LANES).astype(BF16)

        def send_part(k, _, parts=parts, which=which):
            pltpu.make_async_remote_copy(
                src_ref=parts.at[samp], dst_ref=parts.at[samp],
                send_sem=samp_sem.at[0, which], recv_sem=samp_sem.at[1, which],
                device_id={"samp": lax.rem(samp + k, SAMP)}, device_id_type=MESH,
            ).start()
            return 0

        lax.fori_loop(1, SAMP, send_part, 0)

    for which in (0, 1):
        parts, half = part_buf[which], CHUNK_HALF[which]
        seven = parts.at[pl.ds(0, SAMP - 1)]
        pltpu.make_async_copy(seven, seven, samp_sem.at[1, which]).wait()
        for k in (0, 1):
            total = sum(parts[k + 2 * j].astype(F32) for j in range(SAMP // 2)) * SCALE
            for parity in (0, 1):
                for h in (0, 1):
                    at = half * (2 * parity + h)
                    for first, count in CHUNK_TAPS[which]:
                        row = OUT_ROWS * h + 4 * first + 2 * k + parity
                        fin[pl.ds(row, count, stride=4), :] = total[at : at + count]
                        at += count
    for tap in range(TAPS):
        for h in (0, 1):
            row = OUT_ROWS * h + 4 * tap
            w2_out[tap, :, LANES * h : LANES * (h + 1)] = fin[row : row + 4, :]

    halo.wait_send()
    pltpu.make_async_copy(
        crecv.at[most], crecv.at[most], cot_sem.at[0]
    ).wait()
    cx.wait_send()
    wait_act(0, 0)
    wait_act(1, 0)
    for which in (0, 1):
        sent = recv_buf[which].at[most]
        pltpu.make_async_copy(sent, sent, rs_sem.at[0, which]).wait()
        seven = part_buf[which].at[pl.ds(0, SAMP - 1)]
        pltpu.make_async_copy(seven, seven, samp_sem.at[0, which]).wait()


def on_device(volumes, w_first, bias_first, w_second, cotangent):
    any_space = pl.BlockSpec(memory_space=pltpu.HBM)
    vmem = pl.BlockSpec(memory_space=pltpu.VMEM)
    dma = pltpu.SemaphoreType.DMA
    scratch = [
        pltpu.VMEM((4, CIN, 16, LANES), BF16),
        pltpu.VMEM((TAPS * CIN, CH), BF16),
        pltpu.VMEM((CH, K_BACK), BF16),
        pltpu.VMEM((CH, TAPS * CIN - K_BACK), BF16),
        pltpu.VMEM((1, CH), F32),
        pltpu.VMEM((TAPS, FILT, CH), BF16),
        pltpu.VMEM((8, GRP, LANES), BF16),
        pltpu.VMEM((8 * 40, LANES), F32),
        pltpu.VMEM((GRP // 2 * 32, LANES), F32),
        pltpu.VMEM((GRP // 2, 32, LANES), BF16),
        pltpu.VMEM((GRP, 32, LANES), BF16),
        pltpu.VMEM((2, 3, FILT, LANES), BF16),
        pltpu.VMEM((256, 256), BF16),
        pltpu.VMEM((4, 16, CIN, LANES), BF16),
        pltpu.VMEM((4, 4, CIN, LANES), BF16),
        pltpu.VMEM((4, 4, CIN, LANES), BF16),
        pltpu.VMEM((4, CIN, LANES), BF16),
        pltpu.VMEM((4, CH, LANES), BF16),
        pltpu.VMEM((4, CH, LANES), BF16),
        pltpu.VMEM((2, 4, CH, LANES), F32),
        pltpu.VMEM((CH, LANES), F32),
        pltpu.VMEM((2, 4, 4, QUARTER, LANES), BF16),
        pltpu.VMEM((2, 4, 4, QUARTER, LANES), BF16),
        pltpu.VMEM((2, 4, LANES, FILT), BF16),
        pltpu.VMEM((CH * 8, LANES), F32),
        pltpu.VMEM((GRP * 2 * ROWS, LANES), F32),
        pltpu.VMEM((2, GRP, ROWS, LANES), BF16),
        pltpu.VMEM((GRP, ROWS, LANES), BF16),
        pltpu.VMEM((GRP, ROWS, LANES), BF16),
        pltpu.VMEM((SAMP, 4 * CHUNK_HALF[0], LANES), BF16),
        pltpu.VMEM((SAMP, 4 * CHUNK_HALF[1], LANES), BF16),
        pltpu.VMEM((2 * OUT_ROWS, LANES), F32),
        dma((4,)),
        dma((4,)),
        dma((2,)),
        dma((2,)),
        dma((2,)),
        dma((2, 2)),
        dma((2, 2)),
        dma((2, 2)),
    ]

    pre, w2g = pl.pallas_call(
        kernel,
        out_shape=(
            jax.ShapeDtypeStruct((CH, 8, LANES), BF16),
            jax.ShapeDtypeStruct((TAPS, 4, FILT), F32),
        ),
        in_specs=[any_space] * 5,
        out_specs=(vmem, vmem),
        scratch_shapes=scratch,
        compiler_params=pltpu.CompilerParams(
            collective_id=0, has_side_effects=True, vmem_limit_bytes=60 * 1024 * 1024
        ),
        name="layers",
    )(
        volumes[0],
        jnp.transpose(w_first),
        bias_first.reshape(1, CH),
        jnp.transpose(w_second, (1, 0, 2)),
        cotangent[0],
    )
    return pre.reshape(1, CH, 2, 4, LANES), jnp.transpose(w2g, (2, 0, 1))


def solution(mesh):
    placed = (P("samp", None, "grp", None, None), P(), P(), P(), P("samp", "grp", None, None))
    return jax.shard_map(
        on_device,
        mesh=mesh,
        in_specs=placed,
        out_specs=(P("samp", None, "grp", None, None), P(None, None, "grp")),
        check_vma=False,
    )
```

time: 42.8 us -> 43.8 us (1.023)
  Pallas kernels: 38.7 us -> 39.8 us
    pallas_call x1, Pallas kernels: 38.7 us -> 39.8 us  [on_device(): pl.pallas_call(kernel, out_shape=(jax.ShapeDtypeStruct((CH, 8, LANES), BF...]
where the time goes in v3:
time: 43.8 us; the launch traced here: 43.7 us
  Pallas kernels  39.8 us (91%)
  local copies, waits for them, and re-layouts  3.29 us (8%)
  between operations  0.64 us (1%)
    pallas_call x1, Pallas kernels, on_device(): pl.pallas_call(kernel, out_shape=(jax.ShapeDtypeStruct((CH, 8, LANES), BF...  39.8 us
    unnamed x2, local copies, waits for them, and re-layouts  3.29 us

profile of v3, /device:TPU:1, one launch (start us, length us, event | category | flops | bytes accessed | tf_op | source)
XLA Modules:
  0.0 43.7 jit_solution(16047588232878270915)
XLA Ops:
  0.6 39.8 %layers.1 = (bf16[128,8,128]{2,1,0:T(8,128)(2,1)}, f32[27,4,256]{2,1,0:T(4,128)}) custom-call(bf16[64,4,16,128]{3,2,1,0:T(8,128)(2,1)} %bitcast.8, bf16[1728,128]{1,0:T(8,128)(2,1)} %bitcast.9, f32[1,128]{1,0:T(1,128)} %bitcast.13, bf16[27,256,128]{2,1,0:T(8,128)(2,1)} %bitcast.7, bf16[8,32,128]{2,1,0:T(8,128)(2,1)} %bitcast.12), custom_call_target="tpu_custom_call" | custom-call | tf_op jit(solution)/shard_map/layers/pallas_call | solution.py:448
  40.4 1.7 %copy.9 = bf16[1,128,2,4,128]{4,3,2,1,0:T(4,128)(2,1)} copy(bf16[1,128,2,4,128]{4,3,2,1,0:T(4,128)(2,1)} %bitcast.10) | data formatting | bytes 524288
  42.2 1.5 %copy.10 = f32[256,27,4]{0,2,1:T(4,128)} copy(f32[256,27,4]{0,2,1:T(4,128)} %bitcast.11) | data formatting | bytes 221184

commit v4 on v2

--- a/solution.py
+++ b/solution.py
@@ -23,10 +23,10 @@
 COMBOS = [(b, e) for b in (-1, 0, 1) for e in (-1, 0, 1)]
 PHASES = [(0, 0), (0, 1), (1, 0), (1, 1)]
 TAP_ORDER = [t for n in range(9) for t in (18 + n, n)] + [9 + n for n in range(9)]
-SLOTS = 28
-ROWS_A = 64
-ROWS_B = 48
-ROWS = ROWS_A + ROWS_B
+CHUNK_ROWS = (64, 32, 16)
+CHUNK_START = (0, 64, 96)
+CHUNKS = range(len(CHUNK_ROWS))
+ROWS = sum(CHUNK_ROWS)
 K_BACK = 9 * CIN
 SCALE = 1.0 / math.sqrt(32768)
 
@@ -58,16 +58,31 @@
     vol, w1t, bias, w2, cot,
     pre_out, w2_out,
     vbuf, w1tv, w1_back, w1_rest, biasv, w2v, cotv, cstg, cstage, crecv, cotf, cpart,
-    perm, tn, ty, tz, tyz, hsend, hrecv, pre_s, act_own, act_part, carry, cvar, pgf,
-    send_buf, recv_a, recv_b, part_a, part_b,
+    perm, tn, ty, tz, tyz, hsend, hrecv, pre_s, act_own, act_part, carry, cvar, pgf, pre_v,
+    send_buf, recv_a, recv_b, recv_c, part_a, part_b, part_c,
     lsem, vsem, halo_sem, cot_sem, cx_sem, act_sem, rs_sem, samp_sem,
 ):
-    recv_buf = (recv_a, recv_b)
-    part_buf = (part_a, part_b)
+    recv_buf = (recv_a, recv_b, recv_c)
+    part_buf = (part_a, part_b, part_c)
     me = lax.axis_index("grp")
     samp = lax.axis_index("samp")
     core = lax.rem(samp, 2)
     other = samp + 1 - 2 * core
+
+    def peer(j):
+        def step(v):
+            return 2 + lax.div(v * (7 - v), 2)
+
+        z = lax.rem(lax.div(me, 16) + 1 + lax.div(j, 16), 2)
+        x = lax.rem(lax.rem(lax.div(me, 4), 4) + step(lax.rem(lax.div(j, 4), 4)), 4)
+        y = lax.rem(lax.rem(me, 4) + step(lax.rem(j, 4)), 4)
+        return 16 * z + 4 * x + y
+
+    def ring_peer(j):
+        return lax.rem(me + 1 + j, GRP)
+
+    def samp_peer(j):
+        return lax.rem(samp + 4 + j + lax.div(j, 4), SAMP)
 
     ld_cot = pltpu.make_async_copy(cot, cotv, lsem.at[0])
     ld_w1 = pltpu.make_async_copy(w1t, w1tv, lsem.at[1])
@@ -83,20 +98,16 @@
 
     barrier = pltpu.get_barrier_semaphore()
 
-    def greet_grp(k, _):
-        pl.semaphore_signal(
-            barrier, inc=1, device_id={"grp": lax.rem(me + k, GRP)}, device_id_type=MESH
-        )
+    def greet_grp(j, _):
+        pl.semaphore_signal(barrier, inc=1, device_id={"grp": peer(j)}, device_id_type=MESH)
         return 0
 
-    def greet_samp(k, _):
-        pl.semaphore_signal(
-            barrier, inc=1, device_id={"samp": lax.rem(samp + k, SAMP)}, device_id_type=MESH
-        )
+    def greet_samp(j, _):
+        pl.semaphore_signal(barrier, inc=1, device_id={"samp": samp_peer(j)}, device_id_type=MESH)
         return 0
 
-    lax.fori_loop(1, SAMP, greet_samp, 0)
-    lax.fori_loop(1, GRP, greet_grp, 0)
+    lax.fori_loop(0, SAMP - 1, greet_samp, 0)
+    lax.fori_loop(0, GRP - 1, greet_grp, 0)
 
     ld_cot.wait()
     for f in range(8):
@@ -104,26 +115,6 @@
         cstg[pl.ds(f, GRP, stride=16), :] = x
         cstg[pl.ds(8 + f, GRP, stride=16), :] = jnp.concatenate([x[1:], x[:1]], axis=0)
     cstage[...] = cstg[...].reshape(GRP, 16, LANES).astype(BF16)
-
-    pl.semaphore_wait(barrier, GRP - 1 + SAMP - 1)
-
-    halo = pltpu.make_async_remote_copy(
-        src_ref=hsend, dst_ref=hrecv,
-        send_sem=halo_sem.at[0], recv_sem=halo_sem.at[1],
-        device_id={"grp": lax.rem(me + 1, GRP)}, device_id_type=MESH,
-    )
-
-    def send_cot(k, _):
-        dest = lax.rem(me + k, GRP)
-        pltpu.make_async_remote_copy(
-            src_ref=cstage.at[dest], dst_ref=crecv.at[me],
-            send_sem=cot_sem.at[0], recv_sem=cot_sem.at[1],
-            device_id={"grp": dest}, device_id_type=MESH,
-        ).start()
-        return 0
-
-    lax.fori_loop(1, GRP, send_cot, 0)
-    crecv[me] = cstage[me]
 
     ld_w1.wait()
     ld_bias.wait()
@@ -185,6 +176,25 @@
         back = products(w1_back, (3,), pair).astype(BF16)
         hsend[2 * pair] = back[:, :LANES]
         hsend[2 * pair + 1] = back[:, LANES:]
+    pl.semaphore_wait(barrier, GRP - 1 + SAMP - 1)
+
+    halo = pltpu.make_async_remote_copy(
+        src_ref=hsend, dst_ref=hrecv,
+        send_sem=halo_sem.at[0], recv_sem=halo_sem.at[1],
+        device_id={"grp": lax.rem(me + 1, GRP)}, device_id_type=MESH,
+    )
+
+    def send_cot(j, _):
+        dest = peer(j)
+        pltpu.make_async_remote_copy(
+            src_ref=cstage.at[dest], dst_ref=crecv.at[me],
+            send_sem=cot_sem.at[0], recv_sem=cot_sem.at[1],
+            device_id={"grp": dest}, device_id_type=MESH,
+        ).start()
+        return 0
+
+    lax.fori_loop(0, GRP - 1, send_cot, 0)
+    crecv[me] = cstage[me]
     halo.start()
 
     for x in (1, 2):
@@ -248,19 +258,19 @@
         send_buf[:, 1, rows, :] = jnp.concatenate(odd, axis=1).astype(BF16)
 
     def send_chunk(which):
-        rows = pl.ds(0, ROWS_A) if which == 0 else pl.ds(ROWS_A, ROWS_B)
-
-        def body(k, _):
-            dest = lax.rem(me + k, GRP)
+        rows = pl.ds(CHUNK_START[which], CHUNK_ROWS[which])
+
+        def body(j, _):
+            dest = ring_peer(j)
             pltpu.make_async_remote_copy(
                 src_ref=send_buf.at[lax.div(dest, 2), lax.rem(dest, 2), rows],
-                dst_ref=recv_buf[which].at[k - 1],
+                dst_ref=recv_buf[which].at[j],
                 send_sem=rs_sem.at[0, which], recv_sem=rs_sem.at[1, which],
                 device_id={"grp": dest}, device_id_type=MESH,
             ).start()
             return 0
 
-        lax.fori_loop(1, GRP, body, 0)
+        lax.fori_loop(0, GRP - 1, body, 0)
 
     def cot_rhs(p):
         return jnp.concatenate([cotf[p, my_half, :], cpart[p]], axis=1)
@@ -304,8 +314,10 @@
             pack(group, held)
             group += 1
             held = []
+            if group == 6:
+                send_chunk(1)
     pack(group, held + [jnp.zeros((CH, LANES), F32)] * (4 - len(held)))
-    send_chunk(1)
+    send_chunk(2)
 
     ld_w2.wait()
     for i in (0, 1):
@@ -325,43 +337,45 @@
             z = pre_s[i, q]
             g = 1.0 / (1.0 + jnp.exp(-z))
             pgf[pl.ds(4 * i + q, CH, stride=8), :] = grad * (g * (1.0 + z * (1.0 - g)))
-    pre_out[...] = pgf[...].reshape(CH, 8, LANES).astype(BF16)
+    pre_v[...] = pgf[...].reshape(CH, 8, LANES).astype(BF16)
+    st_pre = pltpu.make_async_copy(pre_v, pre_out, lsem.at[4])
+    st_pre.start()
 
     mine = send_buf.at[lax.div(me, 2), lax.rem(me, 2)]
-    chunk_rows = (pl.ds(0, ROWS_A), pl.ds(ROWS_A, ROWS_B))
-    for which in (0, 1):
+    for which in CHUNKS:
         received, parts = recv_buf[which], part_buf[which]
         pltpu.make_async_copy(received, received, rs_sem.at[1, which]).wait()
         parts[samp] = lax.fori_loop(
             0,
             GRP - 1,
             lambda j, acc, received=received: acc + received[j].astype(F32),
-            mine[chunk_rows[which], :].astype(F32),
+            mine[pl.ds(CHUNK_START[which], CHUNK_ROWS[which]), :].astype(F32),
         ).astype(BF16)
 
-        def send_part(k, _, parts=parts, which=which):
+        def send_part(j, _, parts=parts, which=which):
             pltpu.make_async_remote_copy(
                 src_ref=parts.at[samp], dst_ref=parts.at[samp],
                 send_sem=samp_sem.at[0, which], recv_sem=samp_sem.at[1, which],
-                device_id={"samp": lax.rem(samp + k, SAMP)}, device_id_type=MESH,
+                device_id={"samp": samp_peer(j)}, device_id_type=MESH,
             ).start()
             return 0
 
-        lax.fori_loop(1, SAMP, send_part, 0)
-
-    for which in (0, 1):
+        lax.fori_loop(0, SAMP - 1, send_part, 0)
+
+    for which in CHUNKS:
         parts = part_buf[which]
         seven = parts.at[pl.ds(0, SAMP - 1)]
         pltpu.make_async_copy(seven, seven, samp_sem.at[1, which]).wait()
         for h in (0, 1):
             total = sum(parts[h + 2 * j].astype(F32) for j in range(SAMP // 2)) * SCALE
-            first = 0 if which == 0 else ROWS_A // 4
+            first = CHUNK_START[which] // 4
             for slot in range(total.shape[0] // 4):
                 if first + slot < TAPS:
                     w2_out[TAP_ORDER[first + slot], :, LANES * h : LANES * (h + 1)] = total[
                         4 * slot : 4 * slot + 4
                     ]
 
+    st_pre.wait()
     halo.wait_send()
     pltpu.make_async_copy(
         cstage.at[pl.ds(0, GRP - 1)], cstage.at[pl.ds(0, GRP - 1)], cot_sem.at[0]
@@ -369,14 +383,25 @@
     cx.wait_send()
     for c in act_copy:
         c.wait_send()
-    for which in (0, 1):
+    for which in CHUNKS:
         pltpu.make_async_copy(recv_buf[which], recv_buf[which], rs_sem.at[0, which]).wait()
         seven = part_buf[which].at[pl.ds(0, SAMP - 1)]
         pltpu.make_async_copy(seven, seven, samp_sem.at[0, which]).wait()
 
 
+def hand_over(pre, w2g, pre_out, w2_out, sem):
+    copies = [
+        pltpu.make_async_copy(pre, pre_out, sem.at[0]),
+        pltpu.make_async_copy(w2g, w2_out, sem.at[1]),
+    ]
+    for c in copies:
+        c.start()
+    for c in copies:
+        c.wait()
+
+
 def on_device(volumes, w_first, bias_first, w_second, cotangent):
-    any_space = pl.BlockSpec(memory_space=pltpu.HBM)
+    hbm = pl.BlockSpec(memory_space=pltpu.HBM)
     vmem = pl.BlockSpec(memory_space=pltpu.VMEM)
     dma = pltpu.SemaphoreType.DMA
     scratch = [
@@ -405,19 +430,18 @@
         pltpu.VMEM((2, CH, LANES), F32),
         pltpu.VMEM((2, 4, LANES, FILT), BF16),
         pltpu.VMEM((CH * 8, LANES), F32),
+        pltpu.VMEM((CH, 8, LANES), BF16),
         pltpu.VMEM((GRP // 2, 2, ROWS, LANES), BF16),
-        pltpu.VMEM((GRP - 1, ROWS_A, LANES), BF16),
-        pltpu.VMEM((GRP - 1, ROWS_B, LANES), BF16),
-        pltpu.VMEM((SAMP, ROWS_A, LANES), BF16),
-        pltpu.VMEM((SAMP, ROWS_B, LANES), BF16),
-        dma((4,)),
+        *[pltpu.VMEM((GRP - 1, n, LANES), BF16) for n in CHUNK_ROWS],
+        *[pltpu.VMEM((SAMP, n, LANES), BF16) for n in CHUNK_ROWS],
+        dma((5,)),
         dma((4,)),
         dma((2,)),
         dma((2,)),
         dma((2,)),
         dma((2, 2)),
-        dma((2, 2)),
-        dma((2, 2)),
+        dma((2, len(CHUNK_ROWS))),
+        dma((2, len(CHUNK_ROWS))),
     ]
 
     pre, w2g = pl.pallas_call(
@@ -426,8 +450,8 @@
             jax.ShapeDtypeStruct((CH, 8, LANES), BF16),
             jax.ShapeDtypeStruct((TAPS, 4, FILT), F32),
         ),
-        in_specs=[any_space] * 5,
-        out_specs=(vmem, vmem),
+        in_specs=[hbm] * 5,
+        out_specs=(hbm, vmem),
         scratch_shapes=scratch,
         compiler_params=pltpu.CompilerParams(
             collective_id=0, has_side_effects=True, vmem_limit_bytes=60 * 1024 * 1024
@@ -440,6 +464,17 @@
         jnp.transpose(w_second, (1, 0, 2)),
         cotangent[0],
     )
+    pre, w2g = pl.pallas_call(
+        hand_over,
+        out_shape=(
+            jax.ShapeDtypeStruct(pre.shape, pre.dtype),
+            jax.ShapeDtypeStruct(w2g.shape, w2g.dtype),
+        ),
+        in_specs=[vmem, vmem],
+        out_specs=(hbm, hbm),
+        scratch_shapes=[dma((2,))],
+        name="hand_over",
+    )(pre, w2g)
     return pre.reshape(1, CH, 2, 4, LANES), jnp.transpose(w2g, (2, 0, 1))
 
 

time: 42.8 us -> 39.2 us (0.916)
  local copies, waits for them, and re-layouts: 3.29 us -> 0 us
    unnamed x2 -> x0, local copies, waits for them, and re-layouts: 3.29 us -> none
    pallas_call x1, Pallas kernels: 38.7 us -> 36.7 us  [on_device(): pl.pallas_call(kernel, out_shape=(jax.ShapeDtypeStruct((CH, 8, LANES), BF...]
    pallas_call x0 -> x1, Pallas kernels: none -> 1.72 us  [on_device(): pl.pallas_call(hand_over, out_shape=(jax.ShapeDtypeStruct(pre.shape, pre....]
where the time goes in v4:
time: 39.2 us; the launch traced here: 39.1 us
  Pallas kernels  38.4 us (98%)
  between operations  0.64 us (2%)
    pallas_call x1, Pallas kernels, on_device(): pl.pallas_call(kernel, out_shape=(jax.ShapeDtypeStruct((CH, 8, LANES), BF...  36.7 us
    pallas_call x1, Pallas kernels, on_device(): pl.pallas_call(hand_over, out_shape=(jax.ShapeDtypeStruct(pre.shape, pre....  1.72 us

profile of v4, /device:TPU:1, one launch (start us, length us, event | category | flops | bytes accessed | tf_op | source)
XLA Modules:
  0.0 39.1 jit_solution(12251986948135782195)
XLA Ops:
  0.6 36.7 %layers.1 = (bf16[128,8,128]{2,1,0:T(8,128)(2,1)}, f32[27,4,256]{2,1,0:T(4,128)}) custom-call(bf16[64,4,16,128]{3,2,1,0:T(8,128)(2,1)} %bitcast.8, bf16[1728,128]{1,0:T(8,128)(2,1)} %bitcast.9, f32[1,128]{1,0:T(1,128)} %bitcast.11, bf16[27,256,128]{2,1,0:T(8,128)(2,1)} %bitcast.7, bf16[8,32,128]{2,1,0:T(8,128)(2,1)} %bitcast.10), custom_call_target="tpu_custom_call" | custom-call | tf_op jit(solution)/shard_map/layers/pallas_call | solution.py:447
  37.4 1.7 %hand_over.1 = (bf16[128,8,128]{2,1,0:T(8,128)(2,1)}, f32[27,4,256]{2,1,0:T(4,128)}) custom-call(bf16[128,8,128]{2,1,0:T(8,128)(2,1)} %get-tuple-element.6.pre, f32[27,4,256]{2,1,0:T(4,128)} %get-tuple-element.7.w2g), custom_call_target="tpu_custom_call" | custom-call | tf_op jit(solution)/shard_map/hand_over/pallas_call | solution.py:467

commit v5 on v4

--- a/solution.py
+++ b/solution.py
@@ -58,7 +58,7 @@
     vol, w1t, bias, w2, cot,
     pre_out, w2_out,
     vbuf, w1tv, w1_back, w1_rest, biasv, w2v, cotv, cstg, cstage, crecv, cotf, cpart,
-    perm, tn, ty, tz, tyz, hsend, hrecv, pre_s, act_own, act_part, carry, cvar, pgf, pre_v,
+    perm, tn, ty, tz, tyz, hsend, hrecv, pre_s, act_own, act_part, carry, cvar, pgf,
     send_buf, recv_a, recv_b, recv_c, part_a, part_b, part_c,
     lsem, vsem, halo_sem, cot_sem, cx_sem, act_sem, rs_sem, samp_sem,
 ):
@@ -116,6 +116,26 @@
         cstg[pl.ds(8 + f, GRP, stride=16), :] = jnp.concatenate([x[1:], x[:1]], axis=0)
     cstage[...] = cstg[...].reshape(GRP, 16, LANES).astype(BF16)
 
+    pl.semaphore_wait(barrier, GRP - 1 + SAMP - 1)
+
+    halo = pltpu.make_async_remote_copy(
+        src_ref=hsend, dst_ref=hrecv,
+        send_sem=halo_sem.at[0], recv_sem=halo_sem.at[1],
+        device_id={"grp": lax.rem(me + 1, GRP)}, device_id_type=MESH,
+    )
+
+    def send_cot(j, _):
+        dest = peer(j)
+        pltpu.make_async_remote_copy(
+            src_ref=cstage.at[dest], dst_ref=crecv.at[me],
+            send_sem=cot_sem.at[0], recv_sem=cot_sem.at[1],
+            device_id={"grp": dest}, device_id_type=MESH,
+        ).start()
+        return 0
+
+    lax.fori_loop(0, GRP - 1, send_cot, 0)
+    crecv[me] = cstage[me]
+
     ld_w1.wait()
     ld_bias.wait()
     w1_back[...] = jnp.transpose(w1tv[:K_BACK, :])
@@ -176,25 +196,6 @@
         back = products(w1_back, (3,), pair).astype(BF16)
         hsend[2 * pair] = back[:, :LANES]
         hsend[2 * pair + 1] = back[:, LANES:]
-    pl.semaphore_wait(barrier, GRP - 1 + SAMP - 1)
-
-    halo = pltpu.make_async_remote_copy(
-        src_ref=hsend, dst_ref=hrecv,
-        send_sem=halo_sem.at[0], recv_sem=halo_sem.at[1],
-        device_id={"grp": lax.rem(me + 1, GRP)}, device_id_type=MESH,
-    )
-
-    def send_cot(j, _):
-        dest = peer(j)
-        pltpu.make_async_remote_copy(
-            src_ref=cstage.at[dest], dst_ref=crecv.at[me],
-            send_sem=cot_sem.at[0], recv_sem=cot_sem.at[1],
-            device_id={"grp": dest}, device_id_type=MESH,
-        ).start()
-        return 0
-
-    lax.fori_loop(0, GRP - 1, send_cot, 0)
-    crecv[me] = cstage[me]
     halo.start()
 
     for x in (1, 2):
@@ -337,9 +338,7 @@
             z = pre_s[i, q]
             g = 1.0 / (1.0 + jnp.exp(-z))
             pgf[pl.ds(4 * i + q, CH, stride=8), :] = grad * (g * (1.0 + z * (1.0 - g)))
-    pre_v[...] = pgf[...].reshape(CH, 8, LANES).astype(BF16)
-    st_pre = pltpu.make_async_copy(pre_v, pre_out, lsem.at[4])
-    st_pre.start()
+    pre_out[...] = pgf[...].reshape(CH, 8, LANES).astype(BF16)
 
     mine = send_buf.at[lax.div(me, 2), lax.rem(me, 2)]
     for which in CHUNKS:
@@ -375,7 +374,6 @@
                         4 * slot : 4 * slot + 4
                     ]
 
-    st_pre.wait()
     halo.wait_send()
     pltpu.make_async_copy(
         cstage.at[pl.ds(0, GRP - 1)], cstage.at[pl.ds(0, GRP - 1)], cot_sem.at[0]
@@ -430,11 +428,10 @@
         pltpu.VMEM((2, CH, LANES), F32),
         pltpu.VMEM((2, 4, LANES, FILT), BF16),
         pltpu.VMEM((CH * 8, LANES), F32),
-        pltpu.VMEM((CH, 8, LANES), BF16),
         pltpu.VMEM((GRP // 2, 2, ROWS, LANES), BF16),
         *[pltpu.VMEM((GRP - 1, n, LANES), BF16) for n in CHUNK_ROWS],
         *[pltpu.VMEM((SAMP, n, LANES), BF16) for n in CHUNK_ROWS],
-        dma((5,)),
+        dma((4,)),
         dma((4,)),
         dma((2,)),
         dma((2,)),
@@ -447,11 +444,11 @@
     pre, w2g = pl.pallas_call(
         kernel,
         out_shape=(
-            jax.ShapeDtypeStruct((CH, 8, LANES), BF16),
-            jax.ShapeDtypeStruct((TAPS, 4, FILT), F32),
+            pltpu.VMEM((CH, 8, LANES), BF16),
+            pltpu.VMEM((TAPS, 4, FILT), F32),
         ),
         in_specs=[hbm] * 5,
-        out_specs=(hbm, vmem),
+        out_specs=(vmem, vmem),
         scratch_shapes=scratch,
         compiler_params=pltpu.CompilerParams(
             collective_id=0, has_side_effects=True, vmem_limit_bytes=60 * 1024 * 1024
@@ -474,7 +471,10 @@
         out_specs=(hbm, hbm),
         scratch_shapes=[dma((2,))],
         name="hand_over",
-    )(pre, w2g)
+    )(
+        pltpu.with_memory_space_constraint(pre, pltpu.VMEM),
+        pltpu.with_memory_space_constraint(w2g, pltpu.VMEM),
+    )
     return pre.reshape(1, CH, 2, 4, LANES), jnp.transpose(w2g, (2, 0, 1))
 
 

time: 39.2 us -> 37.5 us (0.957)
  Pallas kernels: 38.4 us -> 36.8 us
    pallas_call x1, Pallas kernels: 1.72 us -> 0.75 us  [on_device(): pl.pallas_call(hand_over, out_shape=(jax.ShapeDtypeStruct(pre.shape, pre....]
    pallas_call x1, Pallas kernels: 36.7 us -> 36 us  [on_device(): pl.pallas_call(kernel, out_shape=(pltpu.VMEM((CH, 8, LANES), BF16), pltpu...]
where the time goes in v5:
time: 37.5 us; the launch traced here: 37.4 us
  Pallas kernels  36.8 us (98%)
  between operations  0.64 us (2%)
    pallas_call x1, Pallas kernels, on_device(): pl.pallas_call(kernel, out_shape=(pltpu.VMEM((CH, 8, LANES), BF16), pltpu...  36 us
    pallas_call x1, Pallas kernels, on_device(): pl.pallas_call(hand_over, out_shape=(jax.ShapeDtypeStruct(pre.shape, pre....  0.75 us

profile of v5, /device:TPU:1, one launch (start us, length us, event | category | flops | bytes accessed | tf_op | source)
XLA Modules:
  0.0 37.4 jit_solution(2676757759871172550)
XLA Ops:
  0.6 36.0 %layers.1 = (bf16[128,8,128]{2,1,0:T(8,128)(2,1)S(1)}, f32[27,4,256]{2,1,0:T(4,128)S(1)}) custom-call(bf16[64,4,16,128]{3,2,1,0:T(8,128)(2,1)} %bitcast.8, bf16[1728,128]{1,0:T(8,128)(2,1)} %bitcast.9, f32[1,128]{1,0:T(1,128)} %bitcast.11, bf16[27,256,128]{2,1,0:T(8,128)(2,1)} %bitcast.7, bf16[8,32,128]{2,1,0:T(8,128)(2,1)} %bitcast.10), custom_call_target="tpu_custom_call" | custom-call | tf_op jit(solution)/shard_map/layers/pallas_call | solution.py:444
  36.6 0.8 %hand_over.1 = (bf16[128,8,128]{2,1,0:T(8,128)(2,1)}, f32[27,4,256]{2,1,0:T(4,128)}) custom-call(bf16[128,8,128]{2,1,0:T(8,128)(2,1)S(1)} %get-tuple-element.6.pre, f32[27,4,256]{2,1,0:T(4,128)S(1)} %get-tuple-element.7.w2g), custom_call_target="tpu_custom_call" | custom-call | tf_op jit(solution)/shard_map/hand_over/pallas_call | solution.py:464

commit v6 on v5

--- a/solution.py
+++ b/solution.py
@@ -99,7 +99,7 @@
     barrier = pltpu.get_barrier_semaphore()
 
     def greet_grp(j, _):
-        pl.semaphore_signal(barrier, inc=1, device_id={"grp": peer(j)}, device_id_type=MESH)
+        pl.semaphore_signal(barrier, inc=1, device_id={"grp": ring_peer(j)}, device_id_type=MESH)
         return 0
 
     def greet_samp(j, _):

time: 37.5 us -> 37.4 us (level)
  no operation moved by 1% of the time
where the time goes in v6:
time: 37.4 us
  Pallas kernels  36.7 us (98%)
  between operations  0.64 us (2%)
    pallas_call x1, Pallas kernels, on_device(): pl.pallas_call(kernel, out_shape=(pltpu.VMEM((CH, 8, LANES), BF16), pltpu...  36 us
    pallas_call x1, Pallas kernels, on_device(): pl.pallas_call(hand_over, out_shape=(jax.ShapeDtypeStruct(pre.shape, pre....  0.75 us

profile of v6, /device:TPU:1, one launch (start us, length us, event | category | flops | bytes accessed | tf_op | source)
XLA Modules:
  0.0 37.4 jit_solution(176051972977485675)
XLA Ops:
  0.6 36.0 %layers.1 = (bf16[128,8,128]{2,1,0:T(8,128)(2,1)S(1)}, f32[27,4,256]{2,1,0:T(4,128)S(1)}) custom-call(bf16[64,4,16,128]{3,2,1,0:T(8,128)(2,1)} %bitcast.8, bf16[1728,128]{1,0:T(8,128)(2,1)} %bitcast.9, f32[1,128]{1,0:T(1,128)} %bitcast.11, bf16[27,256,128]{2,1,0:T(8,128)(2,1)} %bitcast.7, bf16[8,32,128]{2,1,0:T(8,128)(2,1)} %bitcast.10), custom_call_target="tpu_custom_call" | custom-call | tf_op jit(solution)/shard_map/layers/pallas_call | solution.py:444
  36.6 0.8 %hand_over.1 = (bf16[128,8,128]{2,1,0:T(8,128)(2,1)}, f32[27,4,256]{2,1,0:T(4,128)}) custom-call(bf16[128,8,128]{2,1,0:T(8,128)(2,1)S(1)} %get-tuple-element.6.pre, f32[27,4,256]{2,1,0:T(4,128)S(1)} %get-tuple-element.7.w2g), custom_call_target="tpu_custom_call" | custom-call | tf_op jit(solution)/shard_map/hand_over/pallas_call | solution.py:464
